TPU v7x, 32 devices: a whole 2x2x4 slice. The times are simulated.
32 devices in a mesh: grp: 2 (over core), row: 16 (over z, y, x).
Axes of the slice: x: 2, y: 2, z: 4, core: 2. Of those that a mesh axis runs over, the one named last changes fastest.
Arguments:
- pair_in: bfloat16 [2, 2, 384, 384, 128], P('grp', None, 'row'), may hold values from -6 to 6
- crop_lengths: int32 [2], replicated, may hold values from 192 to 384, as said below
- in_gain: float32 [2, 128], P('grp'), may hold values from 0.5 to 1.5
- in_bias: float32 [2, 128], P('grp'), may hold values from -3 to 3
- w_proj: bfloat16 [2, 128, 512], P('grp'), may hold values from -0.5 to 0.5
- w_gate: bfloat16 [2, 128, 128], P('grp'), may hold values from -0.5 to 0.5
- w_out: bfloat16 [2, 128, 128], P('grp'), may hold values from -0.5 to 0.5
- out_gain: float32 [2, 128], P('grp'), may hold values from 0.5 to 1.5
- out_bias: float32 [2, 128], P('grp'), may hold values from -3 to 3
- trans_gain: float32 [2, 128], P('grp'), may hold values from 0.5 to 1.5
- trans_bias: float32 [2, 128], P('grp'), may hold values from -3 to 3
- w_up: bfloat16 [2, 128, 512], P('grp'), may hold values from -0.5 to 0.5
- w_down: bfloat16 [2, 512, 128], P('grp'), may hold values from -0.5 to 0.5
- pair_cot: bfloat16 [2, 2, 384, 384, 128], P('grp', None, 'row'), may hold values from -6 to 6
Outputs:
- pair_out: bfloat16 [2, 2, 384, 384, 128], P('grp', None, 'row')
- pair_grad: float32 [2, 2, 384, 384, 128], P('grp', None, 'row')
- in_gain_grad: float32 [2, 128], P('grp')
- in_bias_grad: float32 [2, 128], P('grp')
- proj_grad: float32 [2, 128, 512], P('grp')
- gate_grad: float32 [2, 128, 128], P('grp')
- out_weight_grad: float32 [2, 128, 128], P('grp')
- out_gain_grad: float32 [2, 128], P('grp')
- out_bias_grad: float32 [2, 128], P('grp')
- trans_gain_grad: float32 [2, 128], P('grp')
- trans_bias_grad: float32 [2, 128], P('grp')
- up_grad: float32 [2, 128, 512], P('grp')
- down_grad: float32 [2, 512, 128], P('grp')
Inputs may be any that keep to these rules, and one draw needn't show every extreme that they name: `crop_lengths`: one crop, drawn from the seed, has all 384 residues; positions from a crop's length on are padding.
All inputs are finite; a program needn't handle non-finite values.
Results may differ from a plain program's by a relative error of at most 0.013.
Values may be sent and summed in bfloat16 or wider, within the bound.
No kernel may reach another device: no remote copies, remote signals or barrier semaphores. Data moves between devices by JAX's collectives and lax.ppermute only.
A program may use at most 768 MiB of HBM per device.

v0:
```python
import functools

import jax
import jax.numpy as jnp
from jax import lax
from jax.experimental import pallas as pl
from jax.experimental.pallas import tpu as pltpu
from jax.sharding import PartitionSpec as P

EPSILON = 1e-05
F32 = jnp.float32
BF16 = jnp.bfloat16


def norm_stats(values):
    mean_value = jnp.mean(values, axis=-1, keepdims=True)
    centred = values - mean_value
    inv_scale = lax.rsqrt(jnp.mean(centred * centred, axis=-1, keepdims=True) + EPSILON)
    return (centred * inv_scale, inv_scale)


def norm_back(grad_scaled, scaled, inv_scale):
    mean_grad = jnp.mean(grad_scaled, axis=-1, keepdims=True)
    mean_cross = jnp.mean(grad_scaled * scaled, axis=-1, keepdims=True)
    return inv_scale * (grad_scaled - mean_grad - scaled * mean_cross)


def dot(a, b):
    return jnp.dot(a, b, preferred_element_type=F32)


def dot_t(a, b):
    return jnp.einsum("ijf,cf->ijc", a, b, preferred_element_type=F32)


def outer(a, b):
    return jnp.einsum("ijc,ijf->cf", a, b, preferred_element_type=F32)


def to_channels(value, n):
    rows, cols, channels = value.shape
    return jnp.transpose(value, (2, 0, 1)).reshape(n, channels // n, rows, cols)


def from_channels(value):
    n, held, rows, cols = value.shape
    return jnp.transpose(value.reshape(n * held, rows, cols), (1, 2, 0))


def swap_rows(value):
    return lax.all_to_all(value, "row", 0, 0)


def pre(state, mask, w):
    scaled, _ = norm_stats(state)
    normed = (scaled * w["gain_in"] + w["bias_in"]).astype(BF16)
    projected = dot(normed, w["proj"])
    width = projected.shape[-1] // 4
    lv, lg, rv, rg = (projected[..., i * width : (i + 1) * width] for i in range(4))
    left = (jax.nn.sigmoid(lg) * lv * mask).astype(BF16)
    right = (jax.nn.sigmoid(rg) * rv * mask).astype(BF16)
    return normed, left, right


def post(state, normed, mixed, w):
    gate_logit = dot(normed, w["gate"])
    scaled_mid, inv_mid = norm_stats(mixed)
    mixed_norm = (scaled_mid * w["gain_out"] + w["bias_out"]).astype(BF16)
    update = dot(mixed_norm, w["out"])
    gate_sigma = jax.nn.sigmoid(gate_logit)
    first_state = state + gate_sigma * update
    scaled_tr, inv_tr = norm_stats(first_state)
    trans_normed = (scaled_tr * w["gain_tr"] + w["bias_tr"]).astype(BF16)
    hidden = dot(trans_normed, w["up"])
    activated = jax.nn.silu(hidden).astype(BF16)
    result = (first_state + dot(activated, w["down"])).astype(BF16)
    saved = (gate_sigma, scaled_mid, inv_mid, mixed_norm, update, scaled_tr, inv_tr, trans_normed, hidden, activated)
    return result, saved


def back_upper(grad_final, saved, w):
    gate_sigma, scaled_mid, inv_mid, mixed_norm, update, scaled_tr, inv_tr, trans_normed, hidden, activated = saved
    grads = {}
    grad_trans = grad_final.astype(BF16)
    grads["down"] = outer(activated, grad_trans)
    grad_act = dot_t(grad_trans, w["down"])
    sigma = jax.nn.sigmoid(hidden)
    grad_hidden = (grad_act * sigma * (1.0 + hidden * (1.0 - sigma))).astype(BF16)
    grads["up"] = outer(trans_normed, grad_hidden)
    grad_tnorm = dot_t(grad_hidden, w["up"])
    grads["gain_tr"] = jnp.sum(grad_tnorm * scaled_tr, axis=(0, 1))
    grads["bias_tr"] = jnp.sum(grad_tnorm, axis=(0, 1))
    grad_result = grad_final + norm_back(grad_tnorm * w["gain_tr"], scaled_tr, inv_tr)
    grad_update = (grad_result * gate_sigma).astype(BF16)
    grad_gate = (grad_result * update * gate_sigma * (1.0 - gate_sigma)).astype(BF16)
    grads["out"] = outer(mixed_norm, grad_update)
    grad_norm_mid = dot_t(grad_update, w["out"])
    grads["gain_out"] = jnp.sum(grad_norm_mid * scaled_mid, axis=(0, 1))
    grads["bias_out"] = jnp.sum(grad_norm_mid, axis=(0, 1))
    grad_mixed = norm_back(grad_norm_mid * w["gain_out"], scaled_mid, inv_mid).astype(BF16)
    return grad_result, grad_gate, grad_mixed, grads


def back_lower(state, normed, mask, grad_result, grad_gate, grad_left, grad_right, w):
    scaled_in, inv_in = norm_stats(state)
    projected = dot(normed, w["proj"])
    width = projected.shape[-1] // 4
    lv, lg, rv, rg = (projected[..., i * width : (i + 1) * width] for i in range(4))
    ls = jax.nn.sigmoid(lg)
    rs = jax.nn.sigmoid(rg)
    gl = grad_left.astype(F32) * mask
    gr = grad_right.astype(F32) * mask
    grad_proj = jnp.concatenate(
        [gl * ls, gl * lv * ls * (1.0 - ls), gr * rs, gr * rv * rs * (1.0 - rs)], axis=-1
    ).astype(BF16)
    grads = {"proj": outer(normed, grad_proj), "gate": outer(normed, grad_gate)}
    grad_normed = dot_t(grad_proj, w["proj"]) + dot_t(grad_gate, w["gate"])
    grads["gain_in"] = jnp.sum(grad_normed * scaled_in, axis=(0, 1))
    grads["bias_in"] = jnp.sum(grad_normed, axis=(0, 1))
    return grad_result + norm_back(grad_normed * w["gain_in"], scaled_in, inv_in), grads


def product(left, right):
    n, held, rows, cols = left.shape
    mixed = jnp.einsum("atik,btjk->taibj", left, right, preferred_element_type=F32)
    return jnp.transpose(mixed.reshape(held, n, rows, n * rows), (1, 0, 2, 3)).astype(BF16)


def product_back(grad_mixed, left, right):
    n, held, rows, cols = left.shape
    split = grad_mixed.reshape(n, held, rows, n, rows)
    grad_left = jnp.einsum("atibj,btjk->atik", split, right, preferred_element_type=F32)
    grad_right = jnp.einsum("atibj,atik->btjk", split, left, preferred_element_type=F32)
    return grad_left.astype(BF16), grad_right.astype(BF16)


BLOCK_ROWS = 12
LANES = 128
VMEM = 62 << 20


def sig(x):
    return 0.5 * jnp.tanh(0.5 * x) + 0.5


def mm(a, b, ca=1, cb=0):
    return lax.dot_general(a, b, (((ca,), (cb,)), ((), ())), preferred_element_type=F32)


def col_stats(values):
    centred = values - jnp.mean(values, axis=0, keepdims=True)
    inv_scale = lax.rsqrt(jnp.mean(centred * centred, axis=0, keepdims=True) + EPSILON)
    return centred * inv_scale, inv_scale


def col_back(grad_scaled, scaled, inv_scale):
    mean_grad = jnp.mean(grad_scaled, axis=0, keepdims=True)
    mean_cross = jnp.mean(grad_scaled * scaled, axis=0, keepdims=True)
    return inv_scale * (grad_scaled - mean_grad - scaled * mean_cross)


def fold(values):
    return jnp.sum(values.reshape(values.shape[0] // 8, 8, values.shape[1]), axis=0)


class Step:
    def __init__(self, place, n, rows, held, block_rows, crop, last, used, chunks):
        self.last = last
        self.live = pl.program_id(0) < used if used < chunks else None
        self.n, self.rows, self.held, self.block = n, rows, held, block_rows
        self.row = pl.program_id(1) * block_rows
        self.length, self.base, self.group = place[crop], place[2], place[3]
        column = pl.program_id(0) * LANES + lax.broadcasted_iota(jnp.int32, (1, LANES), 1)
        self.columns = (column < self.length).astype(F32)

    def mask(self, r):
        return self.columns * jnp.where(self.base + self.row + r < self.length, 1.0, 0.0)

    def flat(self, ref):
        return ref[...].reshape(self.block * LANES, ref.shape[-1])

    def pick(self, pair, section):
        own, got = (self.flat(ref).astype(F32) for ref in pair)
        return jnp.where(jnp.full(own.shape, self.group) == section, own, got)

    def put(self, ref, value):
        ref[...] = value.reshape(self.block, LANES, value.shape[-1]).astype(ref.dtype)

    def lanes(self, r):
        return slice(r * LANES, (r + 1) * LANES)

    def spans(self, r):
        return [pl.ds((self.row + r) * self.held + t, self.n, stride=self.rows * self.held) for t in range(self.held)]

    def load(self, scratch, r):
        return jnp.concatenate([scratch[span, :] for span in self.spans(r)], axis=0)

    def store(self, scratch, r, value):
        for t, span in enumerate(self.spans(r)):
            scratch[span, :] = value[t * self.n : (t + 1) * self.n, :]


def unpack(ref, scratch, first=0):
    n, size = ref.shape[0], scratch.shape[0] // (ref.shape[0] + 1)

    def body(d, carry):
        scratch[pl.ds(pl.multiple_of(d * size, 8), size), :] = ref[d, first : first + size, :].astype(F32)
        return carry

    lax.fori_loop(0, n, body, 0)


def pack(scratch, ref, first=0):
    n, size = ref.shape[0], scratch.shape[0] // (ref.shape[0] + 1)

    def body(d, carry):
        ref[d, first : first + size, :] = scratch[pl.ds(pl.multiple_of(d * size, 8), size), :].astype(ref.dtype)
        return carry

    lax.fori_loop(0, n, body, 0)


def fetch(st, ref, scratch, first=0):
    if st.live is None:
        return unpack(ref, scratch, first)

    @pl.when(st.live)
    def _():
        unpack(ref, scratch, first)

    @pl.when(jnp.logical_not(st.live))
    def _():
        scratch[...] = jnp.zeros(scratch.shape, scratch.dtype)


def deliver(st, scratch, ref, first=0):
    if st.live is None:
        return pack(scratch, ref, first)
    pl.when(st.live)(lambda: pack(scratch, ref, first))


def at_first(action):
    pl.when(pl.program_id(1) == 0)(action)


def at_last(action):
    pl.when(pl.program_id(1) == pl.num_programs(1) - 1)(action)


def clear(accs, olds, cols=()):
    @pl.when((pl.program_id(0) == 0) & (pl.program_id(1) == 0))
    def _():
        for k, ref in enumerate(accs):
            ref[...] = olds[k][...] if olds else jnp.zeros(ref.shape, ref.dtype)
        for ref in cols:
            ref[...] = jnp.zeros(ref.shape, ref.dtype)


def add_blocks(ref, first, value):
    for q in range(value.shape[1] // LANES):
        ref[first + q * LANES : first + (q + 1) * LANES, :] += value[:, q * LANES : (q + 1) * LANES]


def close(st, ref, cols=None):
    @pl.when((pl.program_id(0) == pl.num_programs(0) - 1) & (pl.program_id(1) == pl.num_programs(1) - 1))
    def _():
        for k in range(2 if cols is not None else 0):
            row = UP_VEC + 16 + 8 * k
            ref[row : row + 1, :] += jnp.sum(jnp.transpose(cols[k]), axis=0, keepdims=True)
        for q in range(4 if st.last else 0):
            block = slice(q * LANES, (q + 1) * LANES)
            ref[block, :] = jnp.transpose(ref[block, :])


def pre_part(st, state, w, normed_ref, left_scr, right_scr):
    scaled, _ = norm_stats(state)
    normed = (scaled * w.vec[0:1, :] + w.vec[1:2, :]).astype(BF16)
    st.put(normed_ref, normed)
    projected = mm(w.proj_t[...], normed, 1, 1)
    for r in range(st.block):
        lv, lg, rv, rg = (projected[q * LANES : (q + 1) * LANES, st.lanes(r)] for q in range(4))
        mask = st.mask(r)
        st.store(left_scr, r, sig(lg) * lv * mask)
        st.store(right_scr, r, sig(rg) * rv * mask)


def post_part(st, state, normed, mixed_scr, w):
    mids = [col_stats(st.load(mixed_scr, r)) for r in range(st.block)]
    gain, bias = w.col[0], w.col[1]
    mixed_norm = jnp.concatenate([(scaled * gain + bias).astype(BF16) for scaled, _ in mids], axis=1)
    update = mm(mixed_norm, w.out[...], 0, 0)
    gate = sig(mm(normed, w.gate[...]))
    first_state = state + gate * update
    scaled_tr, inv_tr = norm_stats(first_state)
    trans = (scaled_tr * w.vec[2:3, :] + w.vec[3:4, :]).astype(BF16)
    hidden = mm(trans, w.up[...])
    sigma = sig(hidden)
    activated = (hidden * sigma).astype(BF16)
    return mids, mixed_norm, update, gate, first_state, scaled_tr, inv_tr, trans, hidden, sigma, activated


def upper_part(st, grad_final, kept, w, acc, cols, grad_ref, gate_ref, mixed_scr):
    mids, mixed_norm, update, gate, first_state, scaled_tr, inv_tr, trans, hidden, sigma, activated = kept
    low = grad_final.astype(BF16)
    add_blocks(acc, 0, mm(low, activated, 0, 0))
    grad_hidden = (mm(low, w.down[...], 1, 1) * (sigma * (1.0 + hidden * (1.0 - sigma)))).astype(BF16)
    add_blocks(acc, 4 * LANES, mm(trans, grad_hidden, 0, 0))
    grad_tnorm = mm(grad_hidden, w.up[...], 1, 1)
    acc[UP_VEC : UP_VEC + 8, :] += fold(grad_tnorm * scaled_tr)
    acc[UP_VEC + 8 : UP_VEC + 16, :] += fold(grad_tnorm)
    grad_result = grad_final + norm_back(grad_tnorm * w.vec[2:3, :], scaled_tr, inv_tr)
    st.put(grad_ref, grad_result)
    scaled_grad = grad_result * gate
    grad_update = scaled_grad.astype(BF16)
    st.put(gate_ref, scaled_grad * update * (1.0 - gate))
    add_blocks(acc, 8 * LANES, mm(mixed_norm, grad_update))
    grad_norm = mm(w.out[...], grad_update, 1, 1)
    for r, (scaled, inv_scale) in enumerate(mids):
        grad = grad_norm[:, st.lanes(r)]
        cols[0] += grad * scaled
        cols[1] += grad
        st.store(mixed_scr, r, col_back(grad * w.col[0], scaled, inv_scale) * st.mask(r))


def lower_part(st, state, normed, grad_result, grad_gate, left_scr, right_scr, w, acc):
    projected = mm(w.proj_t[...], normed, 1, 1)
    parts = []
    for r in range(st.block):
        lv, lg, rv, rg = (projected[q * LANES : (q + 1) * LANES, st.lanes(r)] for q in range(4))
        ls, rs = sig(lg), sig(rg)
        a, b = st.load(left_scr, r) * ls, st.load(right_scr, r) * rs
        parts.append(jnp.concatenate([v.astype(BF16) for v in (a, a * lv * (1.0 - ls), b, b * rv * (1.0 - rs))], axis=0))
    grad_proj = jnp.concatenate(parts, axis=1)
    acc[: 4 * LANES, :] += mm(grad_proj, normed)
    add_blocks(acc, 4 * LANES, mm(normed, grad_gate, 0, 0))
    grad_normed = jnp.transpose(mm(w.proj[...], grad_proj)) + mm(grad_gate, w.gate[...], 1, 1)
    scaled_in, inv_in = norm_stats(state)
    acc[LOW_VEC : LOW_VEC + 8, :] += fold(grad_normed * scaled_in)
    acc[LOW_VEC + 8 : LOW_VEC + 16, :] += fold(grad_normed)
    return grad_result + norm_back(grad_normed * w.vec[0:1, :], scaled_in, inv_in)


class Weights:
    def __init__(self, group, section, refs, scratch):
        self.wide, self.down, self.vec, self.col, self.proj_t = scratch
        cut = lambda first, count: self.wide.at[:, first * LANES : (first + count) * LANES]
        self.proj, self.gate, self.out, self.up = cut(0, 4), cut(4, 1), cut(5, 1), cut(6, 4)

        @pl.when((pl.program_id(0) == 0) & (pl.program_id(1) == 0))
        def _():
            for chosen, sources in ((group == section, refs[:3]), (group != section, refs[3:])):

                @pl.when(chosen)
                def _():
                    for ref, source in zip((self.wide, self.down, self.vec), sources):
                        ref[...] = source[...]

            for k in range(2):
                self.col[k] = jnp.transpose(jnp.broadcast_to(self.vec[4 + k : 5 + k, :], (LANES, LANES)))
            for q in range(4):
                block = slice(q * LANES, (q + 1) * LANES)
                self.proj_t[block, :] = jnp.transpose(self.wide[:, block])

    @staticmethod
    def scratch():
        return [
            pltpu.VMEM((LANES, 10 * LANES), BF16), pltpu.VMEM((4 * LANES, LANES), BF16), pltpu.VMEM((8, LANES), F32),
            pltpu.VMEM((2, LANES, LANES), F32), pltpu.VMEM((4 * LANES, LANES), BF16),
        ]


def pack_weights(w):
    zero = jnp.zeros_like(w["gain_in"])
    names = ("gain_in", "bias_in", "gain_tr", "bias_tr", "gain_out", "bias_out")
    wide = jnp.concatenate([w[name] for name in ("proj", "gate", "out", "up")], axis=1)
    return wide, w["down"], jnp.stack([w[name] for name in names] + [zero, zero])


UP_VEC = 9 * LANES
UP_ROWS = UP_VEC + 32
LOW_VEC = 5 * LANES
LOW_ROWS = LOW_VEC + 16


def k_pre(cfg, place, own, got, *refs):
    st = Step(place, *cfg)
    w = Weights(st.group, 0, refs[:6], refs[-5:])
    normed, both, left, right = refs[6:-5]
    pre_part(st, st.pick((own, got), 0), w, normed, left, right)

    @at_last
    def _():
        deliver(st, left, both)
        deliver(st, right, both, both.shape[1] // 2)


def k_post_pre(cfg, place, own_0, got_0, own_1, got_1, normed_in, mixed_in, *refs):
    st = Step(place, *cfg)
    w0, w1 = Weights(st.group, 0, refs[:6], refs[-10:-5]), Weights(st.group, 1, refs[:6], refs[-5:])
    *_, home, out, normed, both, mixed, left, right = refs[6:-10]
    at_first(lambda: fetch(st, mixed_in, mixed))
    kept = post_part(st, st.pick((own_0, got_0), 0), st.flat(normed_in), mixed, w0)
    result = (kept[4] + mm(kept[-1], w0.down[...])).astype(BF16)
    st.put(home, result)
    st.put(out, result)
    pre_part(st, result.astype(F32) + st.pick((own_1, got_1), 1), w1, normed, left, right)

    @at_last
    def _():
        deliver(st, left, both)
        deliver(st, right, both, both.shape[1] // 2)


def k_post_upper(cfg, place, own, got, own_cot, got_cot, before, normed_in, mixed_in, *refs):
    st = Step(place, *cfg)
    w = Weights(st.group, 1, refs[:6], refs[-5:])
    _, *olds, home, out, grad, gate, grad_mixed, sums, mixed, cols = refs[6:-5]
    clear([sums], olds, [cols])
    at_first(lambda: fetch(st, mixed_in, mixed))
    state = st.flat(before).astype(F32) + st.pick((own, got), 1)
    kept = post_part(st, state, st.flat(normed_in), mixed, w)
    result = kept[4] + mm(kept[-1], w.down[...])
    st.put(home, result)
    st.put(out, result)
    upper_part(st, st.pick((own_cot, got_cot), 1), kept, w, sums, cols, grad, gate, mixed)
    close(st, sums, cols)
    at_last(lambda: deliver(st, mixed, grad_mixed))


def k_lower_upper(
    cfg, place, own_1, got_1, own_0, got_0, own_cot, got_cot, before, normed_1, grad_1, gate_1, normed_0, both, mixed_in, *refs
):
    st = Step(place, *cfg)
    w1, w0 = Weights(st.group, 1, refs[:6], refs[-10:-5]), Weights(st.group, 0, refs[:6], refs[-5:])
    olds = refs[7:9] if cfg[4] else ()
    home, pair_grad, grad, gate, grad_mixed, low_sums, up_sums, left, right, mixed, cols = refs[-21:-10]
    clear([low_sums, up_sums], olds, [cols])

    @at_first
    def _():
        fetch(st, both, left)
        fetch(st, both, right, both.shape[1] // 2)
        fetch(st, mixed_in, mixed)

    state = st.flat(before).astype(F32) + st.pick((own_1, got_1), 1)
    grad_state = lower_part(
        st, state, st.flat(normed_1), st.flat(grad_1), st.flat(gate_1), left, right, w1, low_sums
    )
    st.put(home, grad_state)
    st.put(pair_grad, grad_state)
    kept = post_part(st, st.pick((own_0, got_0), 0), st.flat(normed_0), mixed, w0)
    grad_final = st.pick((own_cot, got_cot), 0) + grad_state.astype(BF16).astype(F32)
    upper_part(st, grad_final, kept, w0, up_sums, cols, grad, gate, mixed)
    close(st, low_sums)
    close(st, up_sums, cols)
    at_last(lambda: deliver(st, mixed, grad_mixed))


def k_lower(cfg, place, own, got, normed, grad, gate, both, *refs):
    st = Step(place, *cfg)
    w = Weights(st.group, 0, refs[:6], refs[-5:])
    _, *olds, home, pair_grad, sums, parts, left, right = refs[6:-5]
    clear([sums], olds)

    @at_first
    def _():
        fetch(st, both, left)
        fetch(st, both, right, both.shape[1] // 2)

    state = st.pick((own, got), 0)
    grad_state = lower_part(
        st, state, st.flat(normed), st.flat(grad), st.flat(gate), left, right, w, sums
    )
    st.put(home, grad_state)
    st.put(pair_grad, grad_state)
    close(st, sums)

    @pl.when((pl.program_id(0) == pl.num_programs(0) - 1) & (pl.program_id(1) == pl.num_programs(1) - 1))
    def _():
        n, rows, _ = parts.shape
        parts[...] = jnp.zeros(parts.shape, BF16)
        for d in range(n):
            count = max(0, min(rows, LOW_ROWS - d * rows))
            if count:
                parts[d, :count, :] = sums[d * rows : d * rows + count, :].astype(BF16)


def k_results(total, proj, gate, gain_in, bias_in, out, gain_out, bias_out, gain_tr, bias_tr, up, down, early, low):
    n = total.shape[0]
    first, second = early.shape[0] // n, low.shape[0] // n
    for d in range(n):
        early[d * first : (d + 1) * first, :] = total[d, :first, :].astype(F32)
        low[d * second : (d + 1) * second, :] = total[d, first:, :].astype(F32)
    down[0] = early[: 4 * LANES, :]
    for q in range(4):
        up[0, :, q * LANES : (q + 1) * LANES] = early[(4 + q) * LANES : (5 + q) * LANES, :]
        proj[0, :, q * LANES : (q + 1) * LANES] = low[q * LANES : (q + 1) * LANES, :]
    out[0] = early[8 * LANES : UP_VEC, :]
    gate[0] = low[4 * LANES : LOW_VEC, :]
    for k, ref in enumerate((gain_tr, bias_tr, gain_out, bias_out)):
        ref[...] = jnp.sum(early[UP_VEC + 8 * k : UP_VEC + 8 * k + 8, :], axis=0, keepdims=True)
    for k, ref in enumerate((gain_in, bias_in)):
        ref[...] = jnp.sum(low[LOW_VEC + 8 * k : LOW_VEC + 8 * k + 8, :], axis=0, keepdims=True)


def spread(ref, scratch, first=0):
    n, size = ref.shape[0], (scratch.shape[1] - 8) // ref.shape[0]

    def body(d, carry):
        for c in range(scratch.shape[0]):
            value = ref[d, first : first + size, c * LANES : (c + 1) * LANES]
            scratch[c, pl.ds(pl.multiple_of(d * size, 8), size), :] = value.astype(F32)
        return carry

    lax.fori_loop(0, n, body, 0)


def gather(scratch, ref, first=0):
    n, size = ref.shape[0], (scratch.shape[1] - 8) // ref.shape[0]

    def body(d, carry):
        for c in range(scratch.shape[0]):
            value = scratch[c, pl.ds(pl.multiple_of(d * size, 8), size), :]
            ref[d, first : first + size, c * LANES : (c + 1) * LANES] = value.astype(ref.dtype)
        return carry

    lax.fori_loop(0, n, body, 0)


def channel(scratch, t, held):
    chunks, size, _ = scratch.shape
    span = pl.ds(t, (size - 8) // held, stride=held)
    return jnp.concatenate([scratch[c, span, :].astype(BF16) for c in range(chunks)], axis=1)


def put_channel(scratch, t, held, value):
    chunks, size, _ = scratch.shape
    span = pl.ds(t, (size - 8) // held, stride=held)
    for c in range(chunks):
        scratch[c, span, :] = value[:, c * LANES : (c + 1) * LANES]


def k_product(held, both, out, left, right):
    spread(both, left)
    spread(both, right, both.shape[1] // 2)

    def body(t, carry):
        others = channel(right, t, held)[: left.shape[0] * LANES]
        put_channel(left, t, held, mm(channel(left, t, held), others, 1, 1))
        return carry

    lax.fori_loop(0, held, body, 0)
    gather(left, out)


def k_product_back(held, grad_in, both, out, grad, left, right):
    spread(grad_in, grad)
    spread(both, left)
    spread(both, right, both.shape[1] // 2)

    def body(t, carry):
        low, lv, rv = channel(grad, t, held), channel(left, t, held), channel(right, t, held)
        put_channel(left, t, held, mm(low, rv[: low.shape[1]]))
        grad_right = mm(low, lv, 0, 0)
        if low.shape[1] < rv.shape[0]:
            rest = jnp.zeros((rv.shape[0] - low.shape[1], lv.shape[1]), F32)
            grad_right = jnp.concatenate([grad_right, rest])
        put_channel(right, t, held, grad_right)
        return carry

    lax.fori_loop(0, held, body, 0)
    gather(left, out)
    gather(right, out, both.shape[1] // 2)


STEPS = """\
1A SA0 1B SB0 TA0 MA0 TB0 MB0 2A SA1 2B SB1 TA1 MA1 TB1 MB1 3A GA1 3B GB1 tA1 sA1 tB1 sB1 HA HB 4A GA0 4B GB0 tA0 sA0 tB0 sB0 EB0 QB0 5A JA 5B qB0 JB AB0
"""


class Kernels:
    def __init__(self, place, used, n, rows, cols, channels, block_rows):
        self.place, self.used, self.crops = place, used, len(used)
        self.n, self.rows, self.cols, self.channels, self.block = n, rows, cols, channels, block_rows
        self.held = channels // n
        self.size = rows * self.held
        self.chunks = cols // LANES

    def row_call(self, body, crop, ins, outs, scratch, micros, cols=0, sections=1):
        rows, block = self.rows, self.block

        def spec(kind, shape):
            if kind == "own":
                return pl.BlockSpec(
                    (pl.squeezed, block, LANES, shape[-1]), lambda c, i, s: (s[4 + crop], s[3] * (rows // block) + i, c, 0)
                )
            if kind in ("home 0", "home 1"):
                first = int(kind[-1]) * (rows // block)
                return pl.BlockSpec((pl.squeezed, block, LANES, shape[-1]), lambda c, i, s: (s[4 + crop], first + i, c, 0))
            if kind == "rows":
                return pl.BlockSpec((block, LANES, shape[-1]), lambda c, i, s: (i, c, 0))
            if kind == "moved":
                final = shape[-1] // LANES - 1
                return pl.BlockSpec(shape[:-1] + (LANES,), lambda c, i, s: (0, 0, jnp.minimum(c, final)))
            if kind == "kept":
                return pl.BlockSpec(memory_space=pl.ANY)
            zeros = (0,) * len(shape)
            return pl.BlockSpec(shape, lambda c, i, s: zeros)

        aliases = {1 + k: 0 for k, (kind, _) in enumerate(ins) if kind == "kept"}
        return pl.pallas_call(
            functools.partial(
                body, (self.n, rows, self.held, block, crop, crop == self.crops - 1, self.used[crop], self.chunks)
            ),
            out_shape=tuple(v for _, v in outs),
            grid_spec=pltpu.PrefetchScalarGridSpec(
                num_scalar_prefetch=1,
                grid=(self.chunks, rows // block),
                in_specs=[spec(k, v.shape) for k, v in ins],
                out_specs=tuple(spec(k, v.shape) for k, v in outs),
                scratch_shapes=[pltpu.VMEM(((self.n + 1) * self.size, LANES), F32)] * scratch
                + [pltpu.VMEM((2, self.channels, LANES), F32)] * cols
                + Weights.scratch() * sections,
            ),
            input_output_aliases=aliases,
            compiler_params=pltpu.CompilerParams(vmem_limit_bytes=VMEM),
            cost_estimate=cost(micros),
        )(self.place, *[v for _, v in ins])

    def home(self, section, dtype):
        return (f"home {section}", jax.ShapeDtypeStruct((self.crops, 2 * self.rows, self.cols, self.channels), dtype))

    def pairs(self, dtype):
        return ("rows", jax.ShapeDtypeStruct((self.rows, self.cols, self.channels), dtype))

    def moved(self, crop, count=1):
        return ("moved", jax.ShapeDtypeStruct((self.n, count * self.size, self.used[crop] * LANES), BF16))

    def sums(self, rows):
        return ("all", jax.ShapeDtypeStruct((rows, self.channels), F32))

    def channel_call(self, body, ins, out, scratch, micros):
        spec = pl.BlockSpec(memory_space=pltpu.VMEM)
        return pl.pallas_call(
            functools.partial(body, self.held),
            out_shape=out[1],
            in_specs=[spec] * len(ins),
            out_specs=spec,
            scratch_shapes=[pltpu.VMEM((out[1].shape[2] // LANES, self.n * self.size + 8, LANES), F32)] * scratch,
            compiler_params=pltpu.CompilerParams(vmem_limit_bytes=VMEM),
            cost_estimate=cost(micros),
        )(*ins)


def cost(micros):
    return pl.CostEstimate(flops=int(micros * 1.15e9), bytes_accessed=int(micros * 1e6), transcendentals=0)


def steps(kernels, crops, pair, cot, weights, early, late_share, other_half, meet):
    w = [("all", v) for v in weights]
    call, pairs, moved = kernels.row_call, kernels.pairs, kernels.moved
    up_sums, low_sums = kernels.sums(UP_ROWS), kernels.sums(LOW_ROWS)
    earlier = lambda *names: [("all", state[0][name]) for name in names if name in state[0]]
    homes = {}
    kept = lambda name: [("kept", homes[name])]
    mine = lambda v, crop: [("own", v[0]), ("rows", v[1][crop])]
    part = lambda *vs: [("rows", v) for v in vs]
    far = lambda *vs: [("moved", v) for v in vs]
    swap = lambda v: lax.all_to_all(v, ("row", "grp"), 0, 0)
    spread_rows = lambda v: lax.all_to_all(v, "row", 0, 0)
    state = [dict() for _ in range(crops)]
    last = {}

    def ordered(kind, op, value):
        if kind in last:
            value, _ = lax.optimization_barrier((value, last[kind]))
        result = op(value)
        last[kind] = result[0] if isinstance(result, (tuple, list)) else result
        return result

    def row_kernel(body, crop, ins, *rest):
        return ordered("kernel", lambda v: call(body, crop, [(ins[0][0], v)] + ins[1:], *rest), ins[0][1])

    def channel_kernel(body, ins, *rest):
        return ordered("kernel", lambda v: kernels.channel_call(body, (v,) + tuple(ins[1:]), *rest), ins[0])

    def pre(crop, s):
        s["normed_0"], s["both_0"] = row_kernel(k_pre, crop, mine(pair, crop) + w, [pairs(BF16), moved(crop, 2)], 2, 10)

    def post_pre(crop, s):
        homes["out"], s["out_0"], s["normed_1"], s["both_1"] = row_kernel(
            k_post_pre, crop,
            mine(pair, crop) + mine(pair, crop) + part(s["normed_0"]) + far(s["mixed_0"]) + w + (kept("out") if crop else []),
            [kernels.home(0, BF16), pairs(BF16), pairs(BF16), moved(crop, 2)], 3, 18, 0, 2,
        )
        s["got_out_0"] = other_half(s["out_0"], 0)

    def post_upper(crop, s):
        homes["out"], s["out_1"], s["grad_1"], s["gate_1"], s["grad_mixed_1"], s["up_1"] = row_kernel(
            k_post_upper, crop,
            mine(pair, crop) + mine(cot, crop) + part(s["out_0"], s["normed_1"]) + far(s["mixed_1"]) + w + kept("out")
            + earlier("up_1"),
            [kernels.home(1, BF16), pairs(BF16), pairs(F32), pairs(BF16), moved(crop), up_sums], 1, 23, 1,
        )
        s["got_out_1"] = other_half(s["out_1"], 1)

    def lower_upper(crop, s):
        homes["grad"], s["pair_grad_1"], s["grad_0"], s["gate_0"], s["grad_mixed_0"], s["low_1"], s["up_0"] = row_kernel(
            k_lower_upper, crop,
            mine(pair, crop) + mine(pair, crop) + mine(cot, crop)
            + part(s["out_0"], s["normed_1"], s["grad_1"], s["gate_1"], s["normed_0"])
            + far(s["back_1"], s["mixed_0"]) + w + (kept("grad") if crop else []) + earlier("low_1", "up_0"),
            [kernels.home(1, F32), pairs(F32), pairs(F32), pairs(BF16), moved(crop), low_sums, up_sums], 3, 31, 1, 2,
        )
        s["got_grad_1"] = other_half(s["pair_grad_1"], 1)

    def lower(crop, s):
        homes["grad"], s["pair_grad_0"], s["low_0"], s["late"] = row_kernel(
            k_lower, crop, mine(pair, crop) + part(s["normed_0"], s["grad_0"], s["gate_0"]) + far(s["back_0"]) + w
            + kept("grad") + earlier("low_0"),
            [kernels.home(0, F32), pairs(F32), low_sums, ("all", jax.ShapeDtypeStruct(share_shape(LOW_ROWS), BF16))], 2, 13,
        )
        s["got_grad_0"] = other_half(s["pair_grad_0"], 0)

    def product(crop, s, k):
        s[f"product_{k}"] = channel_kernel(k_product, (s[f"factors_{k}"],), moved(crop), 2, 6)

    def product_back(crop, s, k):
        s[f"grads_{k}"] = channel_kernel(k_product_back, (s[f"g_{k}"], s[f"factors_{k}"]), moved(crop, 2), 3, 12)

    transfers = dict(S=("factors", "both"), M=("mixed", "product"), G=("g", "grad_mixed"), s=("back", "grads"))
    rows_of = {"1": pre, "2": post_pre, "3": post_upper, "4": lower_upper, "5": lower}
    channels_of = {"T": product, "t": product_back}
    for step in STEPS.split():
        what, crop, k = step[0], "AB".index(step[1]), step[2:]
        s = state[crop]
        if what == "E":
            sums = {name: lax.optimization_barrier((s[name], last["kernel"]))[0] for name in ("up_0", "up_1", "low_1")}
            last["kernel"] = s["early"] = early(sums)
        elif what in "QqA":
            if what == "A":
                s["total"] = ordered("swap", spread_rows, late_share(s["share_q"], s["share_Q"]))
            else:
                moved_parts = ordered("swap", spread_rows, s["early" if what == "Q" else "late"])
                s[f"share_{what}"] = jnp.sum(moved_parts.astype(F32), axis=0)
        elif what in "HJ":
            name = "out" if what == "H" else "grad"
            homes[name] = meet(homes[name], crop, s[f"got_{name}_0"], s[f"got_{name}_1"])
            if what == "H":
                last["kernel"] = homes[name]
        elif what in rows_of:
            rows_of[what](crop, s)
        elif what in channels_of:
            channels_of[what](crop, s, k)
        else:
            new, old = transfers[what]
            s[f"{new}_{k}"] = ordered("swap", swap, s[f"{old}_{k}"])

    return state, homes


def share_shape(rows):
    n = lax.axis_size("row")
    return (n, -(-rows // (16 * n)) * 16, LANES)


def in_shares(sums):
    n, rows, _ = share_shape(sums.shape[0])
    return jnp.pad(sums, ((0, n * rows - sums.shape[0]), (0, 0))).reshape(n, rows, LANES)


def early_sums(first, swap, sums):
    early_0 = jnp.concatenate([sums["up_0"], jnp.zeros((LOW_ROWS, LANES), F32)])
    early_1 = jnp.concatenate([sums["up_1"], sums["low_1"]])
    early = jnp.where(first, early_0, early_1) + swap(jnp.where(first, early_1, early_0))
    return jnp.concatenate([in_shares(early[:UP_ROWS]), in_shares(early[UP_ROWS:])], axis=1).astype(BF16)


def late_share(first, late, early):
    late = jnp.where(first, late, 0.0) + lax.ppermute(late, "grp", [(1, 0)])
    rows = early.shape[0] - late.shape[0]
    share = jnp.concatenate([early[:rows], early[rows:] + late]).astype(BF16)
    return jnp.broadcast_to(share[None], (lax.axis_size("row"),) + share.shape)


def plain_steps(n, base, crop_length, pair_0, pair_1, cot_0, cot_1, weights):
    rows, cols = pair_0.shape[:2]
    own_rows = base + jnp.arange(rows)
    mask = (own_rows < crop_length).astype(F32)[:, None, None] * (jnp.arange(cols) < crop_length).astype(F32)[None, :, None]

    def send(*values):
        return swap_rows(jnp.stack([to_channels(v, n) for v in values], axis=1))

    w0, w1 = weights
    state_0 = pair_0.astype(F32)
    normed_0, left, right = pre(state_0, mask, w0)
    lr_0 = send(left, right)
    mixed_0 = from_channels(swap_rows(product(lr_0[:, 0], lr_0[:, 1]))).astype(F32)
    out_0, saved_0 = post(state_0, normed_0, mixed_0, w0)
    state_1 = out_0.astype(F32) + pair_1.astype(F32)
    normed_1, left, right = pre(state_1, mask, w1)
    lr_1 = send(left, right)
    mixed_1 = from_channels(swap_rows(product(lr_1[:, 0], lr_1[:, 1]))).astype(F32)
    out_1, saved_1 = post(state_1, normed_1, mixed_1, w1)
    grad_result, grad_gate, grad_mixed, upper_1 = back_upper(cot_1.astype(F32), saved_1, w1)
    gm = send(grad_mixed)
    glr = swap_rows(jnp.stack(product_back(gm[:, 0], lr_1[:, 0], lr_1[:, 1]), axis=1))
    grad_1, lower_1 = back_lower(
        state_1, normed_1, mask, grad_result, grad_gate, from_channels(glr[:, 0]), from_channels(glr[:, 1]), w1
    )
    grad_final = cot_0.astype(F32) + grad_1.astype(BF16).astype(F32)
    grad_result, grad_gate, grad_mixed, upper_0 = back_upper(grad_final, saved_0, w0)
    gm = send(grad_mixed)
    glr = swap_rows(jnp.stack(product_back(gm[:, 0], lr_0[:, 0], lr_0[:, 1]), axis=1))
    grad_0, lower_0 = back_lower(
        state_0, normed_0, mask, grad_result, grad_gate, from_channels(glr[:, 0]), from_channels(glr[:, 1]), w0
    )
    return out_0, out_1, grad_0, grad_1, {**upper_0, **lower_0}, {**upper_1, **lower_1}


ORDER = ("gain_in", "bias_in", "proj", "gate", "out", "gain_out", "bias_out", "gain_tr", "bias_tr", "up", "down")


def per_device(pair_in, crop_lengths, gain_in, bias_in, proj, gate, out, gain_out, bias_out, gain_tr, bias_tr, up, down, pair_cot):
    own_weights = dict(
        gain_in=gain_in[0], bias_in=bias_in[0], proj=proj[0], gate=gate[0], out=out[0], gain_out=gain_out[0],
        bias_out=bias_out[0], gain_tr=gain_tr[0], bias_tr=bias_tr[0], up=up[0], down=down[0],
    )
    groups, count = lax.axis_size("grp"), lax.axis_size("row")
    crops, rows, cols, channels = pair_in.shape[1:]
    group = lax.axis_index("grp")
    first = group == 0
    base = lax.axis_index("row") * rows
    swap = lambda v: lax.ppermute(v, "grp", [(0, 1), (1, 0)])
    pick = lambda v, i: lax.dynamic_index_in_dim(v, i, 0, keepdims=False)
    n = groups * count
    my_rows = rows // 2
    sizes = channels == LANES and out.shape[1] == LANES and up.shape[2] == 4 * LANES and crops == 2 and groups == 2
    if sizes and rows % 2 == 0 and my_rows % BLOCK_ROWS == 0 and cols % LANES == 0 and channels % n == 0 and n % 8 == 0 and (my_rows * (channels // n)) % 16 == 0:
        before_last = (cols // LANES - 1) * LANES
        swapped = crop_lengths[0] <= before_last
        which = [jnp.where(swapped, 1, 0), jnp.where(swapped, 0, 1)]
        lengths = [crop_lengths[crop] for crop in which]
        place = jnp.stack(lengths + [base + group * my_rows, group] + which).astype(jnp.int32)
        def shared(value):
            other = lambda crop: lax.dynamic_slice(value, (crop, (1 - group) * my_rows, 0, 0), (1, my_rows, cols, channels))
            return value, [swap(other(crop)[0]) for crop in which]

        def meet(home, crop, got_0, got_1):
            half = jnp.where(first, got_0, got_1)[None]
            return lax.dynamic_update_slice(home, half, (which[crop], (1 - group) * my_rows, 0, 0))

        def run(used):
            other_half = lambda value, section: lax.ppermute(value, "grp", [(1 - section, section)])
            pair, own = shared(pair_in[0]), pack_weights(own_weights)
            kernels = Kernels(place, used, n, my_rows, cols, channels, BLOCK_ROWS)
            state, homes = steps(
                kernels, crops, pair, shared(pair_cot[0]), own + tuple(swap(v) for v in own), functools.partial(early_sums, first, swap),
                functools.partial(late_share, first), other_half, meet,
            )
            total, _ = lax.optimization_barrier((state[-1]["total"], homes["grad"]))
            spec = pl.BlockSpec(memory_space=pltpu.VMEM)
            order = ("proj", "gate", "gain_in", "bias_in", "out", "gain_out", "bias_out", "gain_tr", "bias_tr", "up", "down")
            arrays = dict(
                gain_in=gain_in, bias_in=bias_in, proj=proj, gate=gate, out=out, gain_out=gain_out, bias_out=bias_out, gain_tr=gain_tr,
                bias_tr=bias_tr, up=up, down=down,
            )
            results = pl.pallas_call(
                k_results,
                out_shape=[jax.ShapeDtypeStruct(arrays[name].shape, F32) for name in order],
                in_specs=[spec],
                out_specs=[spec] * len(order),
                scratch_shapes=[pltpu.VMEM((s[0] * s[1], LANES), F32) for s in (share_shape(UP_ROWS), share_shape(LOW_ROWS))],
                compiler_params=pltpu.CompilerParams(vmem_limit_bytes=VMEM),
            )(total)
            results = dict(zip(order, results))
            return (homes["out"][None], homes["grad"][None]) + tuple(results[name] for name in ORDER)

        chunks = cols // LANES
        if chunks == 1:
            return run((1, 1))
        return lax.cond(lengths[1] <= before_last, lambda: run((chunks, chunks - 1)), lambda: run((chunks, chunks)))

    other_weights = {k: swap(v) for k, v in own_weights.items()}
    weights = [
        {k: jnp.where(first, own_weights[k], other_weights[k]) for k in ORDER},
        {k: jnp.where(first, other_weights[k], own_weights[k]) for k in ORDER},
    ]

    def both(value):
        own, got = pick(value, group), swap(pick(value, 1 - group))
        return jnp.where(first, own, got), jnp.where(first, got, own)

    def home(value_0, value_1):
        own, got = jnp.where(first, value_0, value_1), swap(jnp.where(first, value_1, value_0))
        return jnp.stack([jnp.where(first, own, got), jnp.where(first, got, own)])[None]

    out_0, out_1, grad_0, grad_1, grads_0, grads_1 = plain_steps(
        count, base, pick(crop_lengths, group), *both(pair_in[0]), *both(pair_cot[0]), weights
    )
    pair_out, pair_grad = home(out_0, out_1), home(grad_0, grad_1)
    mine = {k: jnp.where(first, grads_0[k], grads_1[k]) + swap(jnp.where(first, grads_1[k], grads_0[k])) for k in ORDER}
    summed = lax.psum(mine, "row")
    return (pair_out, pair_grad) + tuple(summed[k][None] for k in ORDER)


def solution(mesh):
    pair = P("grp", None, "row", None, None)
    vector, matrix = P("grp", None), P("grp", None, None)
    weights = (vector, vector, matrix, matrix, matrix, vector, vector, vector, vector, matrix, matrix)
    return jax.shard_map(
        per_device,
        mesh=mesh,
        in_specs=(pair, P()) + weights + (pair,),
        out_specs=(pair, pair) + weights,
        check_vma=False,
    )
```

profile of v0, /device:TPU:0, one launch (start us, length us, event | category | flops | bytes accessed | tf_op | source)
XLA Modules:
  0.0 833.8 jit_solution(8834081085075549668)
XLA Ops:
  4.7 827.8 %conditional.1 = (f32[1,128]{1,0:T(1,128)S(1)}, f32[1,128]{1,0:T(1,128)S(1)}, f32[1,128,512]{2,1,0:T(8,128)}, f32[1,128,128]{2,1,0:T(8,128)}, f32[1,128,128]{2,1...) conditional(s32[]{:T(128)} %bitcast.39, ...), branch_computations={%region_0.3_spmd, %region_3.6_spmd} | conditional | flops 301306609664 | bytes 520156032 | solution.py:882
  11.2 7.8 branch_0_fun.19
  19.0 7.3 all-to-all-start
  29.4 7.8 branch_0_fun.20
  37.2 43.7 %all-to-all-done.both = bf16[32,96,384]{2,1,0:T(8,128)(2,1)} async-done(((bf16[32,96,384]{2,1,0:T(8,128)(2,1)}), bf16[32,96,384]{2,1,0:T(8,128)(2,1)}, u32[]{:S(2)}, u32[]{:S(2)}) %all-to-all-start) | async-done | bytes 2359328 | tf_op jit(solution)/shard_map/cond/branch_0_fun/all_to_all | solution.py:669
  90.0 49.5 %all-to-all-done.1.both = bf16[32,96,384]{2,1,0:T(8,128)(2,1)} async-done(((bf16[32,96,384]{2,1,0:T(8,128)(2,1)}), bf16[32,96,384]{2,1,0:T(8,128)(2,1)}, u32[]{:S(2)}, u32[]{:S(2)}) %all-to-all-start.1) | async-done | bytes 2359328 | tf_op jit(solution)/shard_map/cond/branch_0_fun/all_to_all | solution.py:669
  148.6 24.0 %all-to-all-done.2.mixed_in = bf16[32,48,384]{2,1,0:T(8,128)(2,1)S(1)} async-done(((bf16[32,48,384]{2,1,0:T(8,128)(2,1)}), bf16[32,48,384]{2,1,0:T(8,128)(2,1)S(1)}, u32[]{:S(2)}, u32[]{:S(2)}) %all-to-all-start.2) | async-done | bytes 1179680 | tf_op jit(solution)/shard_map/cond/branch_0_fun/all_to_all | solution.py:669
  177.3 15.5 %branch_0_fun.23 = (bf16[2,24,384,128]{3,2,1,0:T(8,128)(2,1)}, bf16[12,384,128]{2,1,0:T(8,128)(2,1)}, bf16[12,384,128]{2,1,0:T(8,128)(2,1)}, bf16[32,96,384]{2,1,0:T(8,128)(2,1)}) custom-call(s32[6]{0:T(128)S(1)} %get-tuple-element.72.place, bf16[2,24,384,128]{3,2,1,0:T(8,128)(2,1)} %bitcast.62, bf16[12,384,128]{2,1,0:T(8,128)(2,1)} %collective-permute-done.got.got_0.got_1, ...), custom_call_target="tpu_custom_call" | custom-call | flops 20700000256 | bytes 18000000 | tf_op jit(solution)/shard_map/cond/branch_0_fun/pallas_call | solution.py:611
  192.8 13.6 %all-to-all-done.3.mixed_in = bf16[32,48,384]{2,1,0:T(8,128)(2,1)S(1)} async-done(((bf16[32,48,384]{2,1,0:T(8,128)(2,1)}), bf16[32,48,384]{2,1,0:T(8,128)(2,1)S(1)}, u32[]{:S(2)}, u32[]{:S(2)}) %all-to-all-start.3) | async-done | bytes 1179680 | tf_op jit(solution)/shard_map/cond/branch_0_fun/all_to_all | solution.py:669
  211.4 15.6 %branch_0_fun.24 = (bf16[2,24,384,128]{3,2,1,0:T(8,128)(2,1)}, bf16[12,384,128]{2,1,0:T(8,128)(2,1)}, bf16[12,384,128]{2,1,0:T(8,128)(2,1)}, bf16[32,96,384]{2,1,0:T(8,128)(2,1)}) custom-call(s32[6]{0:T(128)S(1)} %get-tuple-element.72.place, bf16[2,24,384,128]{3,2,1,0:T(8,128)(2,1)} %bitcast.64, ...), custom_call_target="tpu_custom_call", output_to_operand_aliasing={{0}: (13, {})} | custom-call | flops 20700000256 | bytes 18000000 | tf_op jit(solution)/shard_map/cond/branch_0_fun/pallas_call | solution.py:611
  227.0 38.9 %all-to-all-done.4.both = bf16[32,96,384]{2,1,0:T(8,128)(2,1)} async-done(((bf16[32,96,384]{2,1,0:T(8,128)(2,1)}), bf16[32,96,384]{2,1,0:T(8,128)(2,1)}, u32[]{:S(2)}, u32[]{:S(2)}) %all-to-all-start.4) | async-done | bytes 2359328 | tf_op jit(solution)/shard_map/cond/branch_0_fun/all_to_all | solution.py:669
  275.1 49.4 %all-to-all-done.5.both = bf16[32,96,384]{2,1,0:T(8,128)(2,1)} async-done(((bf16[32,96,384]{2,1,0:T(8,128)(2,1)}), bf16[32,96,384]{2,1,0:T(8,128)(2,1)}, u32[]{:S(2)}, u32[]{:S(2)}) %all-to-all-start.5) | async-done | bytes 2359328 | tf_op jit(solution)/shard_map/cond/branch_0_fun/all_to_all | solution.py:669
  337.4 20.2 %all-to-all-done.6.mixed_in = bf16[32,48,384]{2,1,0:T(8,128)(2,1)S(1)} async-done(((bf16[32,48,384]{2,1,0:T(8,128)(2,1)}), bf16[32,48,384]{2,1,0:T(8,128)(2,1)S(1)}, u32[]{:S(2)}, u32[]{:S(2)}) %all-to-all-start.6) | async-done | bytes 1179680 | tf_op jit(solution)/shard_map/cond/branch_0_fun/all_to_all | solution.py:669
  361.4 21.5 %branch_0_fun.27 = (bf16[2,24,384,128]{3,2,1,0:T(8,128)(2,1)}, bf16[12,384,128]{2,1,0:T(8,128)(2,1)}, f32[12,384,128]{2,1,0:T(8,128)}, bf16[12,384,128]{2,1,0:T(...) custom-call(s32[6]{0:T(128)S(1)} %get-tuple-element.72.place, ...), custom_call_target="tpu_custom_call", output_to_operand_aliasing={{0}: (14, {})} | custom-call | flops 26449999872 | bytes 23000000 | tf_op jit(solution)/shard_map/cond/branch_0_fun/pallas_call | solution.py:611
  382.9 7.6 all-to-all-done.7.mixed_in
  394.4 21.8 %branch_0_fun.28 = (bf16[2,24,384,128]{3,2,1,0:T(8,128)(2,1)}, bf16[12,384,128]{2,1,0:T(8,128)(2,1)}, f32[12,384,128]{2,1,0:T(8,128)}, bf16[12,384,128]{2,1,0:T(...) custom-call(s32[6]{0:T(128)S(1)} %get-tuple-element.72.place, ...), custom_call_target="tpu_custom_call", output_to_operand_aliasing={{0}: (14, {})} | custom-call | flops 26449999872 | bytes 23000000 | tf_op jit(solution)/shard_map/cond/branch_0_fun/pallas_call | solution.py:611
  416.2 7.2 all-to-all-done.8.grad_in
  435.3 21.9 %all-to-all-done.9.grad_in = bf16[32,48,384]{2,1,0:T(8,128)(2,1)S(1)} async-done(((bf16[32,48,384]{2,1,0:T(8,128)(2,1)}), bf16[32,48,384]{2,1,0:T(8,128)(2,1)S(1)}, u32[]{:S(2)}, u32[]{:S(2)}) %all-to-all-start.9) | async-done | bytes 1179680 | tf_op jit(solution)/shard_map/cond/branch_0_fun/all_to_all | solution.py:669
  471.1 7.2 branch_0_fun.31
  478.3 37.2 %all-to-all-done.10.both = bf16[32,96,384]{2,1,0:T(8,128)(2,1)} async-done(((bf16[32,96,384]{2,1,0:T(8,128)(2,1)}), bf16[32,96,384]{2,1,0:T(8,128)(2,1)}, u32[]{:S(2)}, u32[]{:S(2)}) %all-to-all-start.10) | async-done | bytes 2359328 | tf_op jit(solution)/shard_map/cond/branch_0_fun/all_to_all | solution.py:669
  525.2 29.6 %branch_0_fun.30 = (f32[2,24,384,128]{3,2,1,0:T(8,128)}, f32[12,384,128]{2,1,0:T(8,128)}, f32[12,384,128]{2,1,0:T(8,128)}, bf16[12,384,128]{2,1,0:T(8,128)(2,1)}...) custom-call(s32[6]{0:T(128)S(1)} %get-tuple-element.72.place, ...), custom_call_target="tpu_custom_call" | custom-call | flops 35649998848 | bytes 31000000 | tf_op jit(solution)/shard_map/cond/branch_0_fun/pallas_call | solution.py:611
  554.7 19.7 %all-to-all-done.11.both = bf16[32,96,384]{2,1,0:T(8,128)(2,1)} async-done(((bf16[32,96,384]{2,1,0:T(8,128)(2,1)}), bf16[32,96,384]{2,1,0:T(8,128)(2,1)}, u32[]{:S(2)}, u32[]{:S(2)}) %all-to-all-start.11) | async-done | bytes 2359328 | tf_op jit(solution)/shard_map/cond/branch_0_fun/all_to_all | solution.py:669
  578.9 30.1 %branch_0_fun.32 = (f32[2,24,384,128]{3,2,1,0:T(8,128)}, f32[12,384,128]{2,1,0:T(8,128)}, f32[12,384,128]{2,1,0:T(8,128)}, bf16[12,384,128]{2,1,0:T(8,128)(2,1)}...) custom-call(s32[6]{0:T(128)S(1)} %get-tuple-element.72.place, ...), custom_call_target="tpu_custom_call", output_to_operand_aliasing={{0}: (20, {})} | custom-call | flops 35649998848 | bytes 31000000 | tf_op jit(solution)/shard_map/cond/branch_0_fun/pallas_call | solution.py:611
  615.1 7.2 branch_0_fun.33
  622.3 21.9 %all-to-all-done.13.grad_in = bf16[32,48,384]{2,1,0:T(8,128)(2,1)} async-done(((bf16[32,48,384]{2,1,0:T(8,128)(2,1)}), bf16[32,48,384]{2,1,0:T(8,128)(2,1)}, u32[]{:S(2)}, u32[]{:S(2)}) %all-to-all-start.13) | async-done | bytes 1179680 | tf_op jit(solution)/shard_map/cond/branch_0_fun/all_to_all | solution.py:669
  648.0 7.3 branch_0_fun.34
  659.6 42.9 %all-to-all-done.14.both = bf16[32,96,384]{2,1,0:T(8,128)(2,1)} async-done(((bf16[32,96,384]{2,1,0:T(8,128)(2,1)}), bf16[32,96,384]{2,1,0:T(8,128)(2,1)}, u32[]{:S(2)}, u32[]{:S(2)}) %all-to-all-start.14) | async-done | bytes 2359328 | tf_op jit(solution)/shard_map/cond/branch_0_fun/all_to_all | solution.py:669
  707.9 12.4 %branch_0_fun.35 = (f32[2,24,384,128]{3,2,1,0:T(8,128)}, f32[12,384,128]{2,1,0:T(8,128)}, f32[656,128]{1,0:T(8,128)}, bf16[16,48,128]{2,1,0:T(8,128)(2,1)}) custom-call(s32[6]{0:T(128)S(1)} %get-tuple-element.72.place, bf16[2,24,384,128]{3,2,1,0:T(8,128)(2,1)} %bitcast.72, ...), custom_call_target="tpu_custom_call", output_to_operand_aliasing={{0}: (13, {})} | custom-call | flops 14949999616 | bytes 13000000 | tf_op jit(solution)/shard_map/cond/branch_0_fun/pallas_call | solution.py:611
  728.7 32.6 %all-to-all-done.15.both = bf16[32,96,384]{2,1,0:T(8,128)(2,1)} async-done(((bf16[32,96,384]{2,1,0:T(8,128)(2,1)}), bf16[32,96,384]{2,1,0:T(8,128)(2,1)}, u32[]{:S(2)}, u32[]{:S(2)}) %all-to-all-start.15) | async-done | bytes 2359328 | tf_op jit(solution)/shard_map/cond/branch_0_fun/all_to_all | solution.py:669
  766.3 12.6 %branch_0_fun.36 = (f32[2,24,384,128]{3,2,1,0:T(8,128)}, f32[12,384,128]{2,1,0:T(8,128)}, f32[656,128]{1,0:T(8,128)}, bf16[16,48,128]{2,1,0:T(8,128)(2,1)}) custom-call(s32[6]{0:T(128)S(1)} %get-tuple-element.72.place, bf16[2,24,384,128]{3,2,1,0:T(8,128)(2,1)} %bitcast.73, ...), custom_call_target="tpu_custom_call", output_to_operand_aliasing={{0}: (13, {})} | custom-call | flops 14949999616 | bytes 13000000 | tf_op jit(solution)/shard_map/cond/branch_0_fun/pallas_call | solution.py:611
  781.6 15.1 %all_to_all.152 = bf16[16,48,128]{2,1,0:T(8,128)(2,1)S(1)} all-to-all(bf16[16,48,128]{2,1,0:T(8,128)(2,1)} %get-tuple-element.170), channel_id=1, replica_groups=mesh['grp'=2,'row'=16] {'row'}, dimensions={0} | all-to-all | bytes 393216 | tf_op jit(solution)/shard_map/cond/branch_0_fun/all_to_all | solution.py:670
  806.3 13.8 %all-to-all-done.18.total = bf16[16,128,128]{2,1,0:T(8,128)(2,1)S(1)} async-done(((bf16[16,128,128]{2,1,0:T(8,128)(2,1)}), bf16[16,128,128]{2,1,0:T(8,128)(2,1)S(1)}, u32[]{:S(2)}, u32[]{:S(2)}) %all-to-all-start.18) | async-done | bytes 524320 | tf_op jit(solution)/shard_map/cond/branch_0_fun/all_to_all | solution.py:670
  (140 shorter events, 157.9 us)
Async XLA Ops:
  6.7 3.7 collective-permute-start
  7.3 3.1 collective-permute-start.1
  19.0 61.9 %all-to-all-start = ((bf16[32,96,384]{2,1,0:T(8,128)(2,1)}), bf16[32,96,384]{2,1,0:T(8,128)(2,1)}, u32[]{:S(2)}, u32[]{:S(2)}) async-start(bf16[32,96,384]{2,1,0:T(8,128)(2,1)} %get-tuple-element.91), calls=%async_computation | async-start | bytes 4718592 | tf_op jit(solution)/shard_map/cond/branch_0_fun/all_to_all | solution.py:669
  80.8 58.7 %all-to-all-start.1 = ((bf16[32,96,384]{2,1,0:T(8,128)(2,1)}), bf16[32,96,384]{2,1,0:T(8,128)(2,1)}, u32[]{:S(2)}, u32[]{:S(2)}) async-start(bf16[32,96,384]{2,1,0:T(8,128)(2,1)} %get-tuple-element.92), calls=%async_computation.1 | async-start | bytes 4718592 | tf_op jit(solution)/shard_map/cond/branch_0_fun/all_to_all | solution.py:669
  139.5 33.1 %all-to-all-start.2 = ((bf16[32,48,384]{2,1,0:T(8,128)(2,1)}), bf16[32,48,384]{2,1,0:T(8,128)(2,1)S(1)}, u32[]{:S(2)}, u32[]{:S(2)}) async-start(bf16[32,48,384]{2,1,0:T(8,128)(2,1)} %branch_0_fun.21), calls=%async_computation.2 | async-start | bytes 2359296 | tf_op jit(solution)/shard_map/cond/branch_0_fun/all_to_all | solution.py:669
  173.6 32.7 %all-to-all-start.3 = ((bf16[32,48,384]{2,1,0:T(8,128)(2,1)}), bf16[32,48,384]{2,1,0:T(8,128)(2,1)S(1)}, u32[]{:S(2)}, u32[]{:S(2)}) async-start(bf16[32,48,384]{2,1,0:T(8,128)(2,1)} %branch_0_fun.22), calls=%async_computation.3 | async-start | bytes 2359296 | tf_op jit(solution)/shard_map/cond/branch_0_fun/all_to_all | solution.py:669
  207.4 58.5 %all-to-all-start.4 = ((bf16[32,96,384]{2,1,0:T(8,128)(2,1)}), bf16[32,96,384]{2,1,0:T(8,128)(2,1)}, u32[]{:S(2)}, u32[]{:S(2)}) async-start(bf16[32,96,384]{2,1,0:T(8,128)(2,1)} %get-tuple-element.103), calls=%async_computation.4 | async-start | bytes 4718592 | tf_op jit(solution)/shard_map/cond/branch_0_fun/all_to_all | solution.py:669
  265.9 58.6 %all-to-all-start.5 = ((bf16[32,96,384]{2,1,0:T(8,128)(2,1)}), bf16[32,96,384]{2,1,0:T(8,128)(2,1)}, u32[]{:S(2)}, u32[]{:S(2)}) async-start(bf16[32,96,384]{2,1,0:T(8,128)(2,1)} %get-tuple-element.104), calls=%async_computation.5 | async-start | bytes 4718592 | tf_op jit(solution)/shard_map/cond/branch_0_fun/all_to_all | solution.py:669
  324.5 33.1 %all-to-all-start.6 = ((bf16[32,48,384]{2,1,0:T(8,128)(2,1)}), bf16[32,48,384]{2,1,0:T(8,128)(2,1)S(1)}, u32[]{:S(2)}, u32[]{:S(2)}) async-start(bf16[32,48,384]{2,1,0:T(8,128)(2,1)} %branch_0_fun.25), calls=%async_computation.6 | async-start | bytes 2359296 | tf_op jit(solution)/shard_map/cond/branch_0_fun/all_to_all | solution.py:669
  331.8 29.6 %collective-permute-start.5 = (bf16[12,384,128]{2,1,0:T(8,128)(2,1)}, bf16[12,384,128]{2,1,0:T(8,128)(2,1)}, u32[]{:S(2)}, u32[]{:S(2)}) collective-permute-start(bf16[12,384,128]{2,1,0:T(8,128)(2,1)} %get-tuple-element.378), channel_id=1, source_target_pairs={{0,16},{16,0},{1,17},{17,1},{2,18},{18,2},{3,19},{19,3},{4,20},{20... | collective-permute-start | bytes 3538952 | tf_op jit(solution)/shard_map/cond/branch_0_fun/ppermute | solution.py:834
  332.1 62.3 %collective-permute-start.6 = (bf16[12,384,128]{2,1,0:T(8,128)(2,1)}, bf16[12,384,128]{2,1,0:T(8,128)(2,1)}, u32[]{:S(2)}, u32[]{:S(2)}) collective-permute-start(bf16[12,384,128]{2,1,0:T(8,128)(2,1)} %get-tuple-element.377), channel_id=1, source_target_pairs={{0,16},{16,0},{1,17},{17,1},{2,18},{18,2},{3,19},{19,3},{4,20},{20... | collective-permute-start | bytes 3538952 | tf_op jit(solution)/shard_map/cond/branch_0_fun/ppermute | solution.py:834
  357.6 32.8 %all-to-all-start.7 = ((bf16[32,48,384]{2,1,0:T(8,128)(2,1)}), bf16[32,48,384]{2,1,0:T(8,128)(2,1)}, u32[]{:S(2)}, u32[]{:S(2)}) async-start(bf16[32,48,384]{2,1,0:T(8,128)(2,1)} %branch_0_fun.26), calls=%async_computation.7 | async-start | bytes 2359296 | tf_op jit(solution)/shard_map/cond/branch_0_fun/all_to_all | solution.py:669
  390.5 32.9 %all-to-all-start.8 = ((bf16[32,48,384]{2,1,0:T(8,128)(2,1)}), bf16[32,48,384]{2,1,0:T(8,128)(2,1)S(1)}, u32[]{:S(2)}, u32[]{:S(2)}) async-start(bf16[32,48,384]{2,1,0:T(8,128)(2,1)} %get-tuple-element.127), calls=%async_computation.8 | async-start | bytes 2359296 | tf_op jit(solution)/shard_map/cond/branch_0_fun/all_to_all | solution.py:669
  424.4 32.7 %all-to-all-start.9 = ((bf16[32,48,384]{2,1,0:T(8,128)(2,1)}), bf16[32,48,384]{2,1,0:T(8,128)(2,1)S(1)}, u32[]{:S(2)}, u32[]{:S(2)}) async-start(bf16[32,48,384]{2,1,0:T(8,128)(2,1)} %get-tuple-element.130), calls=%async_computation.9 | async-start | bytes 2359296 | tf_op jit(solution)/shard_map/cond/branch_0_fun/all_to_all | solution.py:669
  457.2 58.3 %all-to-all-start.10 = ((bf16[32,96,384]{2,1,0:T(8,128)(2,1)}), bf16[32,96,384]{2,1,0:T(8,128)(2,1)}, u32[]{:S(2)}, u32[]{:S(2)}) async-start(bf16[32,96,384]{2,1,0:T(8,128)(2,1)} %branch_0_fun.29), calls=%async_computation.10 | async-start | bytes 4718592 | tf_op jit(solution)/shard_map/cond/branch_0_fun/all_to_all | solution.py:669
  461.0 58.9 %collective-permute-start.7 = (bf16[12,384,128]{2,1,0:T(8,128)(2,1)}, bf16[12,384,128]{2,1,0:T(8,128)(2,1)}, u32[]{:S(2)}, u32[]{:S(2)}) collective-permute-start(bf16[12,384,128]{2,1,0:T(8,128)(2,1)} %get-tuple-element.110.before), channel_id=1, source_target_pairs={{16,0},{17,1},{18,2},{19,3},{20,4},{21,5},{22,6},{23,7},{24,8},{25... | collective-permute-start | bytes 3538952 | tf_op jit(solution)/shard_map/cond/branch_0_fun/ppermute | solution.py:854
  462.3 60.3 %collective-permute-start.9 = (bf16[12,384,128]{2,1,0:T(8,128)(2,1)}, bf16[12,384,128]{2,1,0:T(8,128)(2,1)}, u32[]{:S(2)}, u32[]{:S(2)}) collective-permute-start(bf16[12,384,128]{2,1,0:T(8,128)(2,1)} %get-tuple-element.115.before), channel_id=1, source_target_pairs={{16,0},{17,1},{18,2},{19,3},{20,4},{21,5},{22,6},{23,7},{24,8},{25... | collective-permute-start | bytes 3538952 | tf_op jit(solution)/shard_map/cond/branch_0_fun/ppermute | solution.py:854
  463.6 56.3 %collective-permute-start.8 = (bf16[12,384,128]{2,1,0:T(8,128)(2,1)}, bf16[12,384,128]{2,1,0:T(8,128)(2,1)}, u32[]{:S(2)}, u32[]{:S(2)}) collective-permute-start(bf16[12,384,128]{2,1,0:T(8,128)(2,1)} %get-tuple-element.121), channel_id=1, source_target_pairs={{0,16},{1,17},{2,18},{3,19},{4,20},{5,21},{6,22},{7,23},{8,24},{9,... | collective-permute-start | bytes 3538952 | tf_op jit(solution)/shard_map/cond/branch_0_fun/ppermute | solution.py:854
  469.7 52.8 %collective-permute-start.10 = (bf16[12,384,128]{2,1,0:T(8,128)(2,1)}, bf16[12,384,128]{2,1,0:T(8,128)(2,1)S(1)}, u32[]{:S(2)}, u32[]{:S(2)}) collective-permute-start(bf16[12,384,128]{2,1,0:T(8,128)(2,1)} %get-tuple-element.122), channel_id=1, source_target_pairs={{0,16},{1,17},{2,18},{3,19},{4,20},{5,21},{6,22},{7,23},{8,24},{9,... | collective-permute-start | bytes 3538952 | tf_op jit(solution)/shard_map/cond/branch_0_fun/ppermute | solution.py:854
  515.5 58.9 %all-to-all-start.11 = ((bf16[32,96,384]{2,1,0:T(8,128)(2,1)}), bf16[32,96,384]{2,1,0:T(8,128)(2,1)}, u32[]{:S(2)}, u32[]{:S(2)}) async-start(bf16[32,96,384]{2,1,0:T(8,128)(2,1)} %branch_0_fun.31), calls=%async_computation.11 | async-start | bytes 4718592 | tf_op jit(solution)/shard_map/cond/branch_0_fun/all_to_all | solution.py:669
  574.4 34.6 %all-to-all-start.12 = ((bf16[32,48,384]{2,1,0:T(8,128)(2,1)}), bf16[32,48,384]{2,1,0:T(8,128)(2,1)S(1)}, u32[]{:S(2)}, u32[]{:S(2)}) async-start(bf16[32,48,384]{2,1,0:T(8,128)(2,1)} %get-tuple-element.143), calls=%async_computation.12 | async-start | bytes 2359296 | tf_op jit(solution)/shard_map/cond/branch_0_fun/all_to_all | solution.py:669
  609.0 35.1 %all-to-all-start.13 = ((bf16[32,48,384]{2,1,0:T(8,128)(2,1)}), bf16[32,48,384]{2,1,0:T(8,128)(2,1)}, u32[]{:S(2)}, u32[]{:S(2)}) async-start(bf16[32,48,384]{2,1,0:T(8,128)(2,1)} %get-tuple-element.144), calls=%async_computation.13 | async-start | bytes 2359296 | tf_op jit(solution)/shard_map/cond/branch_0_fun/all_to_all | solution.py:669
  644.2 58.3 %all-to-all-start.14 = ((bf16[32,96,384]{2,1,0:T(8,128)(2,1)}), bf16[32,96,384]{2,1,0:T(8,128)(2,1)}, u32[]{:S(2)}, u32[]{:S(2)}) async-start(bf16[32,96,384]{2,1,0:T(8,128)(2,1)} %branch_0_fun.33), calls=%async_computation.14 | async-start | bytes 4718592 | tf_op jit(solution)/shard_map/cond/branch_0_fun/all_to_all | solution.py:669
  655.5 3.9 collective-permute-start.11
  655.7 70.5 %collective-permute-start.13 = (f32[12,384,128]{2,1,0:T(8,128)}, f32[12,384,128]{2,1,0:T(8,128)}, u32[]{:S(2)}, u32[]{:S(2)}) collective-permute-start(f32[12,384,128]{2,1,0:T(8,128)} %get-tuple-element.163), channel_id=1, source_target_pairs={{0,16},{1,17},{2,18},{3,19},{4,20},{5,21},{6,22},{7,23},{8,24},{9,... | collective-permute-start | bytes 7077896 | tf_op jit(solution)/shard_map/cond/branch_0_fun/ppermute | solution.py:854
  702.4 58.8 %all-to-all-start.15 = ((bf16[32,96,384]{2,1,0:T(8,128)(2,1)}), bf16[32,96,384]{2,1,0:T(8,128)(2,1)}, u32[]{:S(2)}, u32[]{:S(2)}) async-start(bf16[32,96,384]{2,1,0:T(8,128)(2,1)} %branch_0_fun.34), calls=%async_computation.15 | async-start | bytes 4718592 | tf_op jit(solution)/shard_map/cond/branch_0_fun/all_to_all | solution.py:669
  720.3 6.6 collective-permute-start.12
  721.6 83.0 %collective-permute-start.15 = (f32[12,384,128]{2,1,0:T(8,128)}, f32[12,384,128]{2,1,0:T(8,128)}, u32[]{:S(2)}, u32[]{:S(2)}) collective-permute-start(f32[12,384,128]{2,1,0:T(8,128)} %get-tuple-element.167), channel_id=1, source_target_pairs={{0,16},{1,17},{2,18},{3,19},{4,20},{5,21},{6,22},{7,23},{8,24},{9,... | collective-permute-start | bytes 7077896 | tf_op jit(solution)/shard_map/cond/branch_0_fun/ppermute | solution.py:854
  761.3 20.4 %all-to-all-start.16 = ((bf16[16,128,128]{2,1,0:T(8,128)(2,1)}), bf16[16,128,128]{2,1,0:T(8,128)(2,1)S(1)}, u32[]{:S(2)}, u32[]{:S(2)}) async-start(bf16[16,128,128]{2,1,0:T(8,128)(2,1)} %pad_maximum_fusion), calls=%async_computation.16 | async-start | bytes 1048576 | tf_op jit(solution)/shard_map/cond/branch_0_fun/all_to_all | solution.py:670
  778.9 25.7 %collective-permute-start.14 = (f32[12,384,128]{2,1,0:T(8,128)}, f32[12,384,128]{2,1,0:T(8,128)S(1)}, u32[]{:S(2)}, u32[]{:S(2)}) collective-permute-start(f32[12,384,128]{2,1,0:T(8,128)} %get-tuple-element.166), channel_id=1, source_target_pairs={{16,0},{17,1},{18,2},{19,3},{20,4},{21,5},{22,6},{23,7},{24,8},{25... | collective-permute-start | bytes 7077896 | tf_op jit(solution)/shard_map/cond/branch_0_fun/ppermute | solution.py:854
  796.8 3.1 collective-permute-start.16
  800.8 19.2 %all-to-all-start.18 = ((bf16[16,128,128]{2,1,0:T(8,128)(2,1)}), bf16[16,128,128]{2,1,0:T(8,128)(2,1)S(1)}, u32[]{:S(2)}, u32[]{:S(2)}) async-start(bf16[16,128,128]{2,1,0:T(8,128)(2,1)} %broadcast_in_dim.46), calls=%async_computation.18 | async-start | bytes 1048576 | tf_op jit(solution)/shard_map/cond/branch_0_fun/all_to_all | solution.py:670
  (31 other events, 136.0 us)
where the time goes:
time: 842 us; the launch traced here: 834 us
  waiting for transfers between devices  453 us (54%)
  Pallas kernels  226 us (27%)
  starting transfers between devices  103 us (12%)
  blocking collectives  15.1 us (2%)
  local copies, waits for them, and re-layouts  14.2 us (2%)
  loops' own time  10.2 us (1%)
  other arithmetic  10.1 us (1%)
    all_to_all x16, waiting for transfers between devices, steps(): swap = lambda v: lax.all_to_all(v, ('row', 'grp'), 0, 0)  430 us
    pallas_call x10, Pallas kernels, row_call(): pl.pallas_call(functools.partial(body, (self.n, rows, self.held, block, c...  175 us
    all_to_all x16, starting transfers between devices, steps(): swap = lambda v: lax.all_to_all(v, ('row', 'grp'), 0, 0)  69.2 us
    pallas_call x8, Pallas kernels, channel_call(): pl.pallas_call(functools.partial(body, self.held), out_shape=out[1], in_s...  49.2 us
    ppermute x8, starting transfers between devices, run(): lax.ppermute(value, 'grp', [(1 - section, section)])  20.9 us
  transfers between devices with their start and end apart: 35, of which 21 were waited for; matrix products, arithmetic and copies ran while one was open for 2% of the time, Pallas kernels for 26%

commit v1 on v0

--- a/solution.py
+++ b/solution.py
@@ -877,9 +877,7 @@
             return (homes["out"][None], homes["grad"][None]) + tuple(results[name] for name in ORDER)
 
         chunks = cols // LANES
-        if chunks == 1:
-            return run((1, 1))
-        return lax.cond(lengths[1] <= before_last, lambda: run((chunks, chunks - 1)), lambda: run((chunks, chunks)))
+        return run((chunks, chunks))
 
     other_weights = {k: swap(v) for k, v in own_weights.items()}
     weights = [

time: 842 us -> 829 us (0.985)
  loops' own time: 10.2 us -> 0 us
    another operation x1 -> x0, loops' own time: 10.2 us -> none  [per_device(): lax.cond(lengths[1] <= before_last, lambda: run((chunks, chunks - 1)), la...]
  transfers between devices with their start and end apart: 35 -> 35, of which waited for: 21 -> 20; matrix products, arithmetic and copies ran while one was open for 2% -> 2% of each run, Pallas kernels for 26% -> 26%
where the time goes in v1:
time: 829 us; the launch traced here: 821 us
  waiting for transfers between devices  450 us (54%)
  Pallas kernels  227 us (27%)
  starting transfers between devices  103 us (12%)
  blocking collectives  15.3 us (2%)
  local copies, waits for them, and re-layouts  13.6 us (2%)
  other arithmetic  10.1 us (1%)
    all_to_all x16, waiting for transfers between devices, steps(): swap = lambda v: lax.all_to_all(v, ('row', 'grp'), 0, 0)  429 us
    pallas_call x10, Pallas kernels, row_call(): pl.pallas_call(functools.partial(body, (self.n, rows, self.held, block, c...  176 us
    all_to_all x16, starting transfers between devices, steps(): swap = lambda v: lax.all_to_all(v, ('row', 'grp'), 0, 0)  69.5 us
    pallas_call x8, Pallas kernels, channel_call(): pl.pallas_call(functools.partial(body, self.held), out_shape=out[1], in_s...  49.2 us
    ppermute x8, starting transfers between devices, run(): lax.ppermute(value, 'grp', [(1 - section, section)])  20.8 us
  transfers between devices with their start and end apart: 35, of which 20 were waited for; matrix products, arithmetic and copies ran while one was open for 2% of the time, Pallas kernels for 26%

profile of v1, /device:TPU:0, one launch (start us, length us, event | category | flops | bytes accessed | tf_op | source)
XLA Modules:
  0.0 820.7 jit_solution(3613365511316554122)
XLA Ops:
  8.1 7.9 shard_map.237
  16.0 7.4 all-to-all-start
  26.5 7.9 shard_map.238
  34.4 43.5 %all-to-all-done.both = bf16[32,96,384]{2,1,0:T(8,128)(2,1)} async-done(((bf16[32,96,384]{2,1,0:T(8,128)(2,1)}), bf16[32,96,384]{2,1,0:T(8,128)(2,1)}, u32[]{:S(2)}, u32[]{:S(2)}) %all-to-all-start) | async-done | bytes 2359328 | tf_op jit(solution)/shard_map/all_to_all | solution.py:669
  87.1 49.5 %all-to-all-done.1.both = bf16[32,96,384]{2,1,0:T(8,128)(2,1)} async-done(((bf16[32,96,384]{2,1,0:T(8,128)(2,1)}), bf16[32,96,384]{2,1,0:T(8,128)(2,1)}, u32[]{:S(2)}, u32[]{:S(2)}) %all-to-all-start.1) | async-done | bytes 2359328 | tf_op jit(solution)/shard_map/all_to_all | solution.py:669
  145.7 24.0 %all-to-all-done.2.mixed_in = bf16[32,48,384]{2,1,0:T(8,128)(2,1)S(1)} async-done(((bf16[32,48,384]{2,1,0:T(8,128)(2,1)}), bf16[32,48,384]{2,1,0:T(8,128)(2,1)S(1)}, u32[]{:S(2)}, u32[]{:S(2)}) %all-to-all-start.2) | async-done | bytes 1179680 | tf_op jit(solution)/shard_map/all_to_all | solution.py:669
  174.4 15.7 %shard_map.241 = (bf16[2,24,384,128]{3,2,1,0:T(8,128)(2,1)}, bf16[12,384,128]{2,1,0:T(8,128)(2,1)}, bf16[12,384,128]{2,1,0:T(8,128)(2,1)}, bf16[32,96,384]{2,1,0:T(8,128)(2,1)}) custom-call(s32[6]{0:T(128)} %stack.19.place, bf16[2,24,384,128]{3,2,1,0:T(8,128)(2,1)} %bitcast.39, bf16[12,384,128]{2,1,0:T(8,128)(2,1)} %collective-permute-done.got.got_0.got_1, ...), custom_call_target="tpu_custom_call" | custom-call | flops 20700000256 | bytes 18000000 | tf_op jit(solution)/shard_map/pallas_call | solution.py:611
  190.1 13.4 %all-to-all-done.3.mixed_in = bf16[32,48,384]{2,1,0:T(8,128)(2,1)S(1)} async-done(((bf16[32,48,384]{2,1,0:T(8,128)(2,1)}), bf16[32,48,384]{2,1,0:T(8,128)(2,1)S(1)}, u32[]{:S(2)}, u32[]{:S(2)}) %all-to-all-start.3) | async-done | bytes 1179680 | tf_op jit(solution)/shard_map/all_to_all | solution.py:669
  208.6 15.7 %shard_map.242 = (bf16[2,24,384,128]{3,2,1,0:T(8,128)(2,1)}, bf16[12,384,128]{2,1,0:T(8,128)(2,1)}, bf16[12,384,128]{2,1,0:T(8,128)(2,1)}, bf16[32,96,384]{2,1,0:T(8,128)(2,1)}) custom-call(s32[6]{0:T(128)} %stack.19.place, bf16[2,24,384,128]{3,2,1,0:T(8,128)(2,1)} %bitcast.41, ...), custom_call_target="tpu_custom_call", output_to_operand_aliasing={{0}: (13, {})} | custom-call | flops 20700000256 | bytes 18000000 | tf_op jit(solution)/shard_map/pallas_call | solution.py:611
  224.3 38.8 %all-to-all-done.4.both = bf16[32,96,384]{2,1,0:T(8,128)(2,1)} async-done(((bf16[32,96,384]{2,1,0:T(8,128)(2,1)}), bf16[32,96,384]{2,1,0:T(8,128)(2,1)}, u32[]{:S(2)}, u32[]{:S(2)}) %all-to-all-start.4) | async-done | bytes 2359328 | tf_op jit(solution)/shard_map/all_to_all | solution.py:669
  272.3 49.4 %all-to-all-done.5.both = bf16[32,96,384]{2,1,0:T(8,128)(2,1)} async-done(((bf16[32,96,384]{2,1,0:T(8,128)(2,1)}), bf16[32,96,384]{2,1,0:T(8,128)(2,1)}, u32[]{:S(2)}, u32[]{:S(2)}) %all-to-all-start.5) | async-done | bytes 2359328 | tf_op jit(solution)/shard_map/all_to_all | solution.py:669
  334.7 20.1 %all-to-all-done.6.mixed_in = bf16[32,48,384]{2,1,0:T(8,128)(2,1)S(1)} async-done(((bf16[32,48,384]{2,1,0:T(8,128)(2,1)}), bf16[32,48,384]{2,1,0:T(8,128)(2,1)S(1)}, u32[]{:S(2)}, u32[]{:S(2)}) %all-to-all-start.6) | async-done | bytes 1179680 | tf_op jit(solution)/shard_map/all_to_all | solution.py:669
  358.6 21.6 %shard_map.245 = (bf16[2,24,384,128]{3,2,1,0:T(8,128)(2,1)}, bf16[12,384,128]{2,1,0:T(8,128)(2,1)}, f32[12,384,128]{2,1,0:T(8,128)}, bf16[12,384,128]{2,1,0:T(8,...) custom-call(s32[6]{0:T(128)} %stack.19.place, ...), custom_call_target="tpu_custom_call", output_to_operand_aliasing={{0}: (14, {})} | custom-call | flops 26449999872 | bytes 23000000 | tf_op jit(solution)/shard_map/pallas_call | solution.py:611
  380.3 7.4 all-to-all-done.7.mixed_in
  391.9 21.9 %shard_map.246 = (bf16[2,24,384,128]{3,2,1,0:T(8,128)(2,1)}, bf16[12,384,128]{2,1,0:T(8,128)(2,1)}, f32[12,384,128]{2,1,0:T(8,128)}, bf16[12,384,128]{2,1,0:T(8,...) custom-call(s32[6]{0:T(128)} %stack.19.place, ...), custom_call_target="tpu_custom_call", output_to_operand_aliasing={{0}: (14, {})} | custom-call | flops 26449999872 | bytes 23000000 | tf_op jit(solution)/shard_map/pallas_call | solution.py:611
  413.8 7.1 all-to-all-done.8.grad_in
  425.6 7.2 shard_map.247
  432.8 21.9 %all-to-all-done.9.grad_in = bf16[32,48,384]{2,1,0:T(8,128)(2,1)S(1)} async-done(((bf16[32,48,384]{2,1,0:T(8,128)(2,1)}), bf16[32,48,384]{2,1,0:T(8,128)(2,1)S(1)}, u32[]{:S(2)}, u32[]{:S(2)}) %all-to-all-start.9) | async-done | bytes 1179680 | tf_op jit(solution)/shard_map/all_to_all | solution.py:669
  468.6 7.2 shard_map.249
  475.7 37.3 %all-to-all-done.10.both = bf16[32,96,384]{2,1,0:T(8,128)(2,1)} async-done(((bf16[32,96,384]{2,1,0:T(8,128)(2,1)}), bf16[32,96,384]{2,1,0:T(8,128)(2,1)}, u32[]{:S(2)}, u32[]{:S(2)}) %all-to-all-start.10) | async-done | bytes 2359328 | tf_op jit(solution)/shard_map/all_to_all | solution.py:669
  522.6 29.7 %shard_map.248 = (f32[2,24,384,128]{3,2,1,0:T(8,128)}, f32[12,384,128]{2,1,0:T(8,128)}, f32[12,384,128]{2,1,0:T(8,128)}, bf16[12,384,128]{2,1,0:T(8,128)(2,1)}, ...) custom-call(s32[6]{0:T(128)} %stack.19.place, bf16[2,24,384,128]{3,2,1,0:T(8,128)(2,1)} %bitcast.45, ...), custom_call_target="tpu_custom_call" | custom-call | flops 35649998848 | bytes 31000000 | tf_op jit(solution)/shard_map/pallas_call | solution.py:611
  552.3 19.5 %all-to-all-done.11.both = bf16[32,96,384]{2,1,0:T(8,128)(2,1)} async-done(((bf16[32,96,384]{2,1,0:T(8,128)(2,1)}), bf16[32,96,384]{2,1,0:T(8,128)(2,1)}, u32[]{:S(2)}, u32[]{:S(2)}) %all-to-all-start.11) | async-done | bytes 2359328 | tf_op jit(solution)/shard_map/all_to_all | solution.py:669
  576.1 30.2 %shard_map.250 = (f32[2,24,384,128]{3,2,1,0:T(8,128)}, f32[12,384,128]{2,1,0:T(8,128)}, f32[12,384,128]{2,1,0:T(8,128)}, bf16[12,384,128]{2,1,0:T(8,128)(2,1)}, ...) custom-call(s32[6]{0:T(128)} %stack.19.place, ...), custom_call_target="tpu_custom_call", output_to_operand_aliasing={{0}: (20, {})} | custom-call | flops 35649998848 | bytes 31000000 | tf_op jit(solution)/shard_map/pallas_call | solution.py:611
  612.4 7.2 shard_map.251
  619.6 21.9 %all-to-all-done.13.grad_in = bf16[32,48,384]{2,1,0:T(8,128)(2,1)} async-done(((bf16[32,48,384]{2,1,0:T(8,128)(2,1)}), bf16[32,48,384]{2,1,0:T(8,128)(2,1)}, u32[]{:S(2)}, u32[]{:S(2)}) %all-to-all-start.13) | async-done | bytes 1179680 | tf_op jit(solution)/shard_map/all_to_all | solution.py:669
  645.3 7.3 shard_map.252
  656.8 42.9 %all-to-all-done.14.both = bf16[32,96,384]{2,1,0:T(8,128)(2,1)} async-done(((bf16[32,96,384]{2,1,0:T(8,128)(2,1)}), bf16[32,96,384]{2,1,0:T(8,128)(2,1)}, u32[]{:S(2)}, u32[]{:S(2)}) %all-to-all-start.14) | async-done | bytes 2359328 | tf_op jit(solution)/shard_map/all_to_all | solution.py:669
  705.3 12.5 %shard_map.253 = (f32[2,24,384,128]{3,2,1,0:T(8,128)}, f32[12,384,128]{2,1,0:T(8,128)}, f32[656,128]{1,0:T(8,128)}, bf16[16,48,128]{2,1,0:T(8,128)(2,1)}) custom-call(s32[6]{0:T(128)} %stack.19.place, bf16[2,24,384,128]{3,2,1,0:T(8,128)(2,1)} %bitcast.49, ...), custom_call_target="tpu_custom_call", output_to_operand_aliasing={{0}: (13, {})} | custom-call | flops 14949999616 | bytes 13000000 | tf_op jit(solution)/shard_map/pallas_call | solution.py:611
  726.2 32.5 %all-to-all-done.15.both = bf16[32,96,384]{2,1,0:T(8,128)(2,1)} async-done(((bf16[32,96,384]{2,1,0:T(8,128)(2,1)}), bf16[32,96,384]{2,1,0:T(8,128)(2,1)}, u32[]{:S(2)}, u32[]{:S(2)}) %all-to-all-start.15) | async-done | bytes 2359328 | tf_op jit(solution)/shard_map/all_to_all | solution.py:669
  763.7 12.8 %shard_map.254 = (f32[2,24,384,128]{3,2,1,0:T(8,128)}, f32[12,384,128]{2,1,0:T(8,128)}, f32[656,128]{1,0:T(8,128)}, bf16[16,48,128]{2,1,0:T(8,128)(2,1)}) custom-call(s32[6]{0:T(128)} %stack.19.place, bf16[2,24,384,128]{3,2,1,0:T(8,128)(2,1)} %bitcast.50, ...), custom_call_target="tpu_custom_call", output_to_operand_aliasing={{0}: (13, {})} | custom-call | flops 14949999616 | bytes 13000000 | tf_op jit(solution)/shard_map/pallas_call | solution.py:611
  779.0 15.3 %all_to_all.95 = bf16[16,48,128]{2,1,0:T(8,128)(2,1)S(1)} all-to-all(bf16[16,48,128]{2,1,0:T(8,128)(2,1)} %get-tuple-element.187), channel_id=1, replica_groups=mesh['grp'=2,'row'=16] {'row'}, dimensions={0} | all-to-all | bytes 393216 | tf_op jit(solution)/shard_map/all_to_all | solution.py:670
  803.9 13.8 %all-to-all-done.18.total = bf16[16,128,128]{2,1,0:T(8,128)(2,1)S(1)} async-done(((bf16[16,128,128]{2,1,0:T(8,128)(2,1)}), bf16[16,128,128]{2,1,0:T(8,128)(2,1)S(1)}, u32[]{:S(2)}, u32[]{:S(2)}) %all-to-all-start.18) | async-done | bytes 524320 | tf_op jit(solution)/shard_map/all_to_all | solution.py:670
  (139 shorter events, 147.9 us)
Async XLA Ops:
  3.4 3.9 collective-permute-start
  4.0 3.3 collective-permute-start.1
  4.1 3.2 collective-permute-start.2
  16.0 61.9 %all-to-all-start = ((bf16[32,96,384]{2,1,0:T(8,128)(2,1)}), bf16[32,96,384]{2,1,0:T(8,128)(2,1)}, u32[]{:S(2)}, u32[]{:S(2)}) async-start(bf16[32,96,384]{2,1,0:T(8,128)(2,1)} %get-tuple-element.110), calls=%async_computation | async-start | bytes 4718592 | tf_op jit(solution)/shard_map/all_to_all | solution.py:669
  77.9 58.7 %all-to-all-start.1 = ((bf16[32,96,384]{2,1,0:T(8,128)(2,1)}), bf16[32,96,384]{2,1,0:T(8,128)(2,1)}, u32[]{:S(2)}, u32[]{:S(2)}) async-start(bf16[32,96,384]{2,1,0:T(8,128)(2,1)} %get-tuple-element.111), calls=%async_computation.1 | async-start | bytes 4718592 | tf_op jit(solution)/shard_map/all_to_all | solution.py:669
  136.6 33.1 %all-to-all-start.2 = ((bf16[32,48,384]{2,1,0:T(8,128)(2,1)}), bf16[32,48,384]{2,1,0:T(8,128)(2,1)S(1)}, u32[]{:S(2)}, u32[]{:S(2)}) async-start(bf16[32,48,384]{2,1,0:T(8,128)(2,1)} %shard_map.239), calls=%async_computation.2 | async-start | bytes 2359296 | tf_op jit(solution)/shard_map/all_to_all | solution.py:669
  170.7 32.7 %all-to-all-start.3 = ((bf16[32,48,384]{2,1,0:T(8,128)(2,1)}), bf16[32,48,384]{2,1,0:T(8,128)(2,1)S(1)}, u32[]{:S(2)}, u32[]{:S(2)}) async-start(bf16[32,48,384]{2,1,0:T(8,128)(2,1)} %shard_map.240), calls=%async_computation.3 | async-start | bytes 2359296 | tf_op jit(solution)/shard_map/all_to_all | solution.py:669
  204.5 58.6 %all-to-all-start.4 = ((bf16[32,96,384]{2,1,0:T(8,128)(2,1)}), bf16[32,96,384]{2,1,0:T(8,128)(2,1)}, u32[]{:S(2)}, u32[]{:S(2)}) async-start(bf16[32,96,384]{2,1,0:T(8,128)(2,1)} %get-tuple-element.122), calls=%async_computation.4 | async-start | bytes 4718592 | tf_op jit(solution)/shard_map/all_to_all | solution.py:669
  263.1 58.6 %all-to-all-start.5 = ((bf16[32,96,384]{2,1,0:T(8,128)(2,1)}), bf16[32,96,384]{2,1,0:T(8,128)(2,1)}, u32[]{:S(2)}, u32[]{:S(2)}) async-start(bf16[32,96,384]{2,1,0:T(8,128)(2,1)} %get-tuple-element.123), calls=%async_computation.5 | async-start | bytes 4718592 | tf_op jit(solution)/shard_map/all_to_all | solution.py:669
  321.7 33.1 %all-to-all-start.6 = ((bf16[32,48,384]{2,1,0:T(8,128)(2,1)}), bf16[32,48,384]{2,1,0:T(8,128)(2,1)S(1)}, u32[]{:S(2)}, u32[]{:S(2)}) async-start(bf16[32,48,384]{2,1,0:T(8,128)(2,1)} %shard_map.243), calls=%async_computation.6 | async-start | bytes 2359296 | tf_op jit(solution)/shard_map/all_to_all | solution.py:669
  329.1 29.5 %collective-permute-start.5 = (bf16[12,384,128]{2,1,0:T(8,128)(2,1)}, bf16[12,384,128]{2,1,0:T(8,128)(2,1)}, u32[]{:S(2)}, u32[]{:S(2)}) collective-permute-start(bf16[12,384,128]{2,1,0:T(8,128)(2,1)} %get-tuple-element.202), channel_id=1, source_target_pairs={{0,16},{16,0},{1,17},{17,1},{2,18},{18,2},{3,19},{19,3},{4,20},{20... | collective-permute-start | bytes 3538952 | tf_op jit(solution)/shard_map/ppermute | solution.py:834
  329.3 62.6 %collective-permute-start.6 = (bf16[12,384,128]{2,1,0:T(8,128)(2,1)}, bf16[12,384,128]{2,1,0:T(8,128)(2,1)}, u32[]{:S(2)}, u32[]{:S(2)}) collective-permute-start(bf16[12,384,128]{2,1,0:T(8,128)(2,1)} %get-tuple-element.201), channel_id=1, source_target_pairs={{0,16},{16,0},{1,17},{17,1},{2,18},{18,2},{3,19},{19,3},{4,20},{20... | collective-permute-start | bytes 3538952 | tf_op jit(solution)/shard_map/ppermute | solution.py:834
  354.8 32.8 %all-to-all-start.7 = ((bf16[32,48,384]{2,1,0:T(8,128)(2,1)}), bf16[32,48,384]{2,1,0:T(8,128)(2,1)}, u32[]{:S(2)}, u32[]{:S(2)}) async-start(bf16[32,48,384]{2,1,0:T(8,128)(2,1)} %shard_map.244), calls=%async_computation.7 | async-start | bytes 2359296 | tf_op jit(solution)/shard_map/all_to_all | solution.py:669
  387.7 33.2 %all-to-all-start.8 = ((bf16[32,48,384]{2,1,0:T(8,128)(2,1)}), bf16[32,48,384]{2,1,0:T(8,128)(2,1)S(1)}, u32[]{:S(2)}, u32[]{:S(2)}) async-start(bf16[32,48,384]{2,1,0:T(8,128)(2,1)} %get-tuple-element.144), calls=%async_computation.8 | async-start | bytes 2359296 | tf_op jit(solution)/shard_map/all_to_all | solution.py:669
  422.0 32.7 %all-to-all-start.9 = ((bf16[32,48,384]{2,1,0:T(8,128)(2,1)}), bf16[32,48,384]{2,1,0:T(8,128)(2,1)S(1)}, u32[]{:S(2)}, u32[]{:S(2)}) async-start(bf16[32,48,384]{2,1,0:T(8,128)(2,1)} %get-tuple-element.147), calls=%async_computation.9 | async-start | bytes 2359296 | tf_op jit(solution)/shard_map/all_to_all | solution.py:669
  454.7 58.3 %all-to-all-start.10 = ((bf16[32,96,384]{2,1,0:T(8,128)(2,1)}), bf16[32,96,384]{2,1,0:T(8,128)(2,1)}, u32[]{:S(2)}, u32[]{:S(2)}) async-start(bf16[32,96,384]{2,1,0:T(8,128)(2,1)} %shard_map.247), calls=%async_computation.10 | async-start | bytes 4718592 | tf_op jit(solution)/shard_map/all_to_all | solution.py:669
  458.5 58.8 %collective-permute-start.7 = (bf16[12,384,128]{2,1,0:T(8,128)(2,1)}, bf16[12,384,128]{2,1,0:T(8,128)(2,1)}, u32[]{:S(2)}, u32[]{:S(2)}) collective-permute-start(bf16[12,384,128]{2,1,0:T(8,128)(2,1)} %get-tuple-element.128.before), channel_id=1, source_target_pairs={{16,0},{17,1},{18,2},{19,3},{20,4},{21,5},{22,6},{23,7},{24,8},{25... | collective-permute-start | bytes 3538952 | tf_op jit(solution)/shard_map/ppermute | solution.py:854
  459.8 60.2 %collective-permute-start.9 = (bf16[12,384,128]{2,1,0:T(8,128)(2,1)}, bf16[12,384,128]{2,1,0:T(8,128)(2,1)}, u32[]{:S(2)}, u32[]{:S(2)}) collective-permute-start(bf16[12,384,128]{2,1,0:T(8,128)(2,1)} %get-tuple-element.133.before), channel_id=1, source_target_pairs={{16,0},{17,1},{18,2},{19,3},{20,4},{21,5},{22,6},{23,7},{24,8},{25... | collective-permute-start | bytes 3538952 | tf_op jit(solution)/shard_map/ppermute | solution.py:854
  461.1 56.2 %collective-permute-start.8 = (bf16[12,384,128]{2,1,0:T(8,128)(2,1)}, bf16[12,384,128]{2,1,0:T(8,128)(2,1)}, u32[]{:S(2)}, u32[]{:S(2)}) collective-permute-start(bf16[12,384,128]{2,1,0:T(8,128)(2,1)} %get-tuple-element.138), channel_id=1, source_target_pairs={{0,16},{1,17},{2,18},{3,19},{4,20},{5,21},{6,22},{7,23},{8,24},{9,... | collective-permute-start | bytes 3538952 | tf_op jit(solution)/shard_map/ppermute | solution.py:854
  467.2 52.8 %collective-permute-start.10 = (bf16[12,384,128]{2,1,0:T(8,128)(2,1)}, bf16[12,384,128]{2,1,0:T(8,128)(2,1)S(1)}, u32[]{:S(2)}, u32[]{:S(2)}) collective-permute-start(bf16[12,384,128]{2,1,0:T(8,128)(2,1)} %get-tuple-element.139), channel_id=1, source_target_pairs={{0,16},{1,17},{2,18},{3,19},{4,20},{5,21},{6,22},{7,23},{8,24},{9,... | collective-permute-start | bytes 3538952 | tf_op jit(solution)/shard_map/ppermute | solution.py:854
  513.0 58.8 %all-to-all-start.11 = ((bf16[32,96,384]{2,1,0:T(8,128)(2,1)}), bf16[32,96,384]{2,1,0:T(8,128)(2,1)}, u32[]{:S(2)}, u32[]{:S(2)}) async-start(bf16[32,96,384]{2,1,0:T(8,128)(2,1)} %shard_map.249), calls=%async_computation.11 | async-start | bytes 4718592 | tf_op jit(solution)/shard_map/all_to_all | solution.py:669
  571.8 34.5 %all-to-all-start.12 = ((bf16[32,48,384]{2,1,0:T(8,128)(2,1)}), bf16[32,48,384]{2,1,0:T(8,128)(2,1)S(1)}, u32[]{:S(2)}, u32[]{:S(2)}) async-start(bf16[32,48,384]{2,1,0:T(8,128)(2,1)} %get-tuple-element.160), calls=%async_computation.12 | async-start | bytes 2359296 | tf_op jit(solution)/shard_map/all_to_all | solution.py:669
  606.3 35.1 %all-to-all-start.13 = ((bf16[32,48,384]{2,1,0:T(8,128)(2,1)}), bf16[32,48,384]{2,1,0:T(8,128)(2,1)}, u32[]{:S(2)}, u32[]{:S(2)}) async-start(bf16[32,48,384]{2,1,0:T(8,128)(2,1)} %get-tuple-element.161), calls=%async_computation.13 | async-start | bytes 2359296 | tf_op jit(solution)/shard_map/all_to_all | solution.py:669
  641.5 58.3 %all-to-all-start.14 = ((bf16[32,96,384]{2,1,0:T(8,128)(2,1)}), bf16[32,96,384]{2,1,0:T(8,128)(2,1)}, u32[]{:S(2)}, u32[]{:S(2)}) async-start(bf16[32,96,384]{2,1,0:T(8,128)(2,1)} %shard_map.251), calls=%async_computation.14 | async-start | bytes 4718592 | tf_op jit(solution)/shard_map/all_to_all | solution.py:669
  652.7 3.9 collective-permute-start.11
  653.0 70.8 %collective-permute-start.13 = (f32[12,384,128]{2,1,0:T(8,128)}, f32[12,384,128]{2,1,0:T(8,128)}, u32[]{:S(2)}, u32[]{:S(2)}) collective-permute-start(f32[12,384,128]{2,1,0:T(8,128)} %get-tuple-element.180), channel_id=1, source_target_pairs={{0,16},{1,17},{2,18},{3,19},{4,20},{5,21},{6,22},{7,23},{8,24},{9,... | collective-permute-start | bytes 7077896 | tf_op jit(solution)/shard_map/ppermute | solution.py:854
  699.8 58.9 %all-to-all-start.15 = ((bf16[32,96,384]{2,1,0:T(8,128)(2,1)}), bf16[32,96,384]{2,1,0:T(8,128)(2,1)}, u32[]{:S(2)}, u32[]{:S(2)}) async-start(bf16[32,96,384]{2,1,0:T(8,128)(2,1)} %shard_map.252), calls=%async_computation.15 | async-start | bytes 4718592 | tf_op jit(solution)/shard_map/all_to_all | solution.py:669
  717.9 6.6 collective-permute-start.12
  719.2 83.0 %collective-permute-start.15 = (f32[12,384,128]{2,1,0:T(8,128)}, f32[12,384,128]{2,1,0:T(8,128)}, u32[]{:S(2)}, u32[]{:S(2)}) collective-permute-start(f32[12,384,128]{2,1,0:T(8,128)} %get-tuple-element.184), channel_id=1, source_target_pairs={{0,16},{1,17},{2,18},{3,19},{4,20},{5,21},{6,22},{7,23},{8,24},{9,... | collective-permute-start | bytes 7077896 | tf_op jit(solution)/shard_map/ppermute | solution.py:854
  758.7 20.4 %all-to-all-start.16 = ((bf16[16,128,128]{2,1,0:T(8,128)(2,1)}), bf16[16,128,128]{2,1,0:T(8,128)(2,1)S(1)}, u32[]{:S(2)}, u32[]{:S(2)}) async-start(bf16[16,128,128]{2,1,0:T(8,128)(2,1)} %pad_maximum_fusion), calls=%async_computation.16 | async-start | bytes 1048576 | tf_op jit(solution)/shard_map/all_to_all | solution.py:670
  776.5 25.7 %collective-permute-start.14 = (f32[12,384,128]{2,1,0:T(8,128)}, f32[12,384,128]{2,1,0:T(8,128)S(1)}, u32[]{:S(2)}, u32[]{:S(2)}) collective-permute-start(f32[12,384,128]{2,1,0:T(8,128)} %get-tuple-element.183), channel_id=1, source_target_pairs={{16,0},{17,1},{18,2},{19,3},{20,4},{21,5},{22,6},{23,7},{24,8},{25... | collective-permute-start | bytes 7077896 | tf_op jit(solution)/shard_map/ppermute | solution.py:854
  798.4 19.2 %all-to-all-start.18 = ((bf16[16,128,128]{2,1,0:T(8,128)(2,1)}), bf16[16,128,128]{2,1,0:T(8,128)(2,1)S(1)}, u32[]{:S(2)}, u32[]{:S(2)}) async-start(bf16[16,128,128]{2,1,0:T(8,128)(2,1)} %broadcast_in_dim.36), calls=%async_computation.18 | async-start | bytes 1048576 | tf_op jit(solution)/shard_map/all_to_all | solution.py:670
  (31 other events, 143.6 us)
